TPU v7x, 32 devices: a whole 2x2x4 slice. The times are simulated.
32 devices in a mesh: member: 2 (over x), gx: 16 (over z, y, core).
Axes of the slice: x: 2, y: 2, z: 4, core: 2. Of those that a mesh axis runs over, the one named last changes fastest.
Arguments:
- analysis: bfloat16 [3, 4, 1536, 512], P(None, None, 'gx'), may hold values from -4 to 4
- zonal_waves: int32 [8, 16], P('member'), parts along dimension 0, may hold values from 0 to 511
- meridional_waves: int32 [8, 16], P('member'), parts along dimension 0, may hold values from 0 to 1535
- amplitude_codes: int32 [8, 16], P('member'), parts along dimension 0, may hold values from 1 to 8
Outputs:
- forecast: bfloat16 [6, 4, 512, 1536], P('member', None, 'gx'), parts along dimension 0
There are 2 independent parts, one for each index of `member`. A program takes and returns all parts, laid end to end along the dimension named above; an argument that names none is the same for every part. Nothing has to cross between parts.
All inputs are finite; a program needn't handle non-finite values.
Results may differ from a plain program's by a relative error of at most 0.006.
Values may be sent and summed in bfloat16 or wider, within the bound.
A program may use at most 64 MiB of HBM per device.

v0:
```python
import functools
import math

import jax
import jax.numpy as jnp
import numpy as np
from jax import lax
from jax.experimental import pallas as pl
from jax.experimental.pallas import tpu as pltpu
from jax.sharding import PartitionSpec as P

STEPS = 4
HALO = 2 * STEPS
TIME_STEP = 0.15
FILTER = 0.03
AMP_UNIT = 0.04
LANES = 128
MESH = pl.DeviceIdType.MESH


def ceil_to(value, unit):
    return -(-value // unit) * unit


def gather_kernel(n, members, x_ref, out_ref, send_ref, send_sem, recv_sem, fsend_sem, frecv_sem):
    comps, levels, own, nx = x_ref.shape
    width = nx // n
    total = out_ref.shape[1]
    half = ceil_to(own // 2, 16)
    me = lax.axis_index("gx")
    member = lax.axis_index("member")
    parity = lax.rem(member, 2)
    partner = member + 1 - 2 * parity

    barrier = pltpu.get_barrier_semaphore()
    for off in range(1, n):
        pl.semaphore_signal(
            barrier, inc=1, device_id=(member, lax.rem(me + off, n)), device_id_type=MESH
        )
    pl.semaphore_signal(barrier, inc=1, device_id=(partner, me), device_id_type=MESH)

    def columns(c, l, first, count):
        first = first % nx
        return x_ref[c, l, :, first : first + count]

    for t in range(n):
        for c in range(comps):
            main = [columns(c, l, t * width, width) for l in range(levels)]
            send_ref[t, c * own : (c + 1) * own, :] = jnp.concatenate(main, axis=1)
            edges = []
            for l in range(levels):
                edges.append(columns(c, l, t * width - HALO, HALO))
                edges.append(columns(c, l, (t + 1) * width, HALO))
            edge = jnp.concatenate(edges, axis=1)
            packed = jnp.concatenate([edge[:half], edge[own - half :]], axis=1)
            start = comps * own + c * half
            send_ref[t, start : start + half, :] = packed
    out_ref[me] = send_ref[me]
    pl.semaphore_wait(barrier, n)

    cut = ceil_to(total // 2, 16)
    parts = (pl.ds(0, cut), pl.ds(cut, total - cut))

    def exchange(mine, other):
        def spread(off):
            target = lax.rem(me + off, n)
            return pltpu.make_async_remote_copy(
                src_ref=send_ref.at[target, mine],
                dst_ref=out_ref.at[me, mine],
                send_sem=send_sem.at[off],
                recv_sem=recv_sem.at[off],
                device_id=(member, target),
                device_id_type=MESH,
            )

        def arrival(off):
            source = lax.rem(me + n - off, n)
            return pltpu.make_async_remote_copy(
                src_ref=send_ref.at[source, mine],
                dst_ref=out_ref.at[source, mine],
                send_sem=send_sem.at[off],
                recv_sem=recv_sem.at[off],
                device_id=(member, source),
                device_id_type=MESH,
            )

        def forward(off, rows):
            source = lax.rem(me + n - off, n)
            return pltpu.make_async_remote_copy(
                src_ref=out_ref.at[source, rows],
                dst_ref=out_ref.at[source, rows],
                send_sem=fsend_sem.at[off],
                recv_sem=frecv_sem.at[off],
                device_id=(partner, me),
                device_id_type=MESH,
            )

        for off in range(1, n):
            spread(off).start()
        for off in range(1, n):
            arrival(off).wait_recv()
            forward(off, mine).start()
        for off in range(1, n):
            forward(off, other).wait_recv()
        for off in range(1, n):
            spread(off).wait_send()
            forward(off, mine).wait_send()

    @pl.when(parity == 0)
    def _():
        exchange(parts[0], parts[1])

    @pl.when(parity == 1)
    def _():
        exchange(parts[1], parts[0])


def gather(analysis, n, members):
    comps, levels, own, nx = analysis.shape
    half = ceil_to(own // 2, 16)
    total = comps * (own + half)
    return pl.pallas_call(
        functools.partial(gather_kernel, n, members),
        out_shape=jax.ShapeDtypeStruct((n, total, LANES), jnp.bfloat16),
        in_specs=[pl.BlockSpec(memory_space=pltpu.VMEM)],
        out_specs=pl.BlockSpec(memory_space=pltpu.VMEM),
        scratch_shapes=[pltpu.VMEM((n, total, LANES), jnp.bfloat16)]
        + [pltpu.SemaphoreType.DMA((n,)) for _ in range(4)],
        compiler_params=pltpu.CompilerParams(
            collective_id=0, has_side_effects=True, vmem_limit_bytes=24 * 2**20
        ),
    )(analysis)


def placing(levels, width):
    wide = width + 2 * HALO
    table = np.zeros((levels * wide, 2 * LANES), np.float32)
    for l in range(levels):
        for x in range(wide):
            row = l * wide + x
            if HALO <= x < HALO + width:
                table[row, l * width + x - HALO] = 1.0
            else:
                e = x if x < HALO else x - width
                lane = l * 2 * HALO + e
                table[row, LANES + lane] = 1.0
                table[row, LANES + LANES // 2 + lane] = 1.0
    return table


def stencils(levels, wide):
    out = wide - 4
    one = {
        "mid": (0, 0, 1, 0, 0),
        "slope": (1, -8, 0, 8, -1),
        "smooth": (1, -4, 6, -4, 1),
    }
    mats = {}
    for name, taps in one.items():
        m = np.zeros((out, wide), np.float32)
        for x in range(out):
            m[x, x : x + 5] = taps
        mats[name] = m
    eye = np.eye(levels, dtype=np.float32)
    k = np.arange(levels)
    mix = 0.25 + 0.25 * (k[None, :] >= k[:, None]).astype(np.float32)
    mid, slope, smooth = (np.kron(eye, mats[s]) for s in ("mid", "slope", "smooth"))
    wind = np.concatenate([mid, slope, smooth])
    thick = np.concatenate([mid, np.kron(mix, mats["slope"]), smooth, np.kron(mix, mats["mid"])])
    flux = np.concatenate([slope, slope], axis=1)
    return wind, thick, flux


def steps_kernel(dims, r_ref, place_ref, left_ref, right_ref, geo_ref, *refs):
    n, comps, levels, own, half, width = dims
    mats = refs[: 3 * STEPS]
    out_ref = refs[3 * STEPS]
    state_ref, hu_ref, wu_ref, wv_ref, wh_ref, wf_ref = refs[3 * STEPS + 1 :]
    ny = n * own
    wide = width + 2 * HALO
    rows = levels * wide
    pad = wu_ref.shape[1]

    row_index = lax.broadcasted_iota(jnp.int32, (n, 2 * half, LANES), 1)
    lane_index = lax.broadcasted_iota(jnp.int32, (n, 2 * half, LANES), 2)
    keep = (row_index < half) == (lane_index < LANES // 2)
    added = jnp.dot(
        left_ref[...],
        right_ref[...],
        preferred_element_type=jnp.float32,
        precision=lax.Precision.HIGHEST,
    )
    for c in range(comps):
        main = r_ref[:, c * own : (c + 1) * own, :]
        start = comps * own + c * half
        edge = r_ref[:, start : start + half, :]
        both = jnp.concatenate([edge, edge], axis=1)
        both = jnp.where(keep, both, jnp.zeros_like(both))
        if 2 * half > own:
            both = jnp.concatenate(
                [both[:, : own - half], both[:, half:]], axis=1
            )
        block = jnp.concatenate([main, both], axis=2).reshape(ny, 2 * LANES)
        field = lax.dot_general(
            place_ref[...], block, (((1,), (1,)), ((), ())), preferred_element_type=jnp.float32
        )
        if c == 0:
            field = field + added
        state_ref[c, :rows, :] = field.astype(jnp.bfloat16)

    for ref in (wu_ref, wv_ref, wh_ref):
        ref[:, ny:] = jnp.zeros((ref.shape[0], pad - ny), jnp.float32)

    for step in range(STEPS):
        rows_in = levels * (wide - 4 * step)
        rows_out = levels * (wide - 4 * step - 4)
        wind, thick, flux = mats[3 * step : 3 * step + 3]
        product = state_ref[0, :rows_in, :].astype(jnp.float32) * state_ref[
            1, :rows_in, :
        ].astype(jnp.float32)
        high = product.astype(jnp.bfloat16)
        hu_ref[:rows_in, :] = high
        hu_ref[rows_in : 2 * rows_in, :] = (product - high.astype(jnp.float32)).astype(jnp.bfloat16)

        def times(m_ref, x, into):
            into[: m_ref.shape[0], :ny] = jnp.dot(
                m_ref[...], x, preferred_element_type=jnp.float32
            )

        times(wind, state_ref[1, :rows_in, :], wu_ref)
        times(wind, state_ref[2, :rows_in, :], wv_ref)
        times(thick, state_ref[0, :rows_in, :], wh_ref)
        times(flux, hu_ref[: 2 * rows_in, :], wf_ref)

        def group(g, carry, rows_out=rows_out, last=step == STEPS - 1):
            size = 16

            def part(ref, which, lanes=ny):
                first = pl.multiple_of(which * rows_out + g * size, size)
                return ref[pl.ds(first, size), :lanes]

            def around(x):
                return [pltpu.roll(x, s % pad, 1) for s in (2, 1, -1, -2)]

            def slope(near):
                return (8.0 * (near[2] - near[1]) - (near[3] - near[0]))[:, :ny]

            def fourth(x, near):
                return ((near[0] + near[3]) - 4.0 * (near[1] + near[2]) + 6.0 * x)[:, :ny]

            inv = geo_ref[0:1, :]
            cor = geo_ref[1:2, :]
            h, u, v, p = (
                part(wh_ref, 0, pad),
                part(wu_ref, 0, pad),
                part(wv_ref, 0, pad),
                part(wh_ref, 3, pad),
            )
            ha, ua, va = around(h), around(u), around(v)
            flux_y = slope([a + a * b for a, b in zip(va, ha)])
            press_y = slope(around(p))
            h_s, u_s, v_s = fourth(h, ha), fourth(u, ua), fourth(v, va)
            u_y, v_y = slope(ua), slope(va)
            h, u, v = h[:, :ny], u[:, :ny], v[:, :ny]
            u_x, v_x = part(wu_ref, 1), part(wv_ref, 1)
            ur = u * inv
            k = TIME_STEP / 12.0
            new_h = (
                h
                - k * (inv * (u_x + part(wf_ref, 0)) + flux_y)
                - FILTER * (h_s + part(wh_ref, 2))
            )
            new_u = (
                u
                - k * (ur * u_x + v * u_y + inv * part(wh_ref, 1))
                + cor * v
                - FILTER * (u_s + part(wu_ref, 2))
            )
            new_v = (
                v
                - k * (ur * v_x + v * v_y + press_y)
                - cor * u
                - FILTER * (v_s + part(wv_ref, 2))
            )
            here = pl.ds(pl.multiple_of(g * size, size), size)
            target = out_ref if last else state_ref
            for c, value in enumerate((new_h, new_u, new_v)):
                target[c, here, :] = value.astype(jnp.bfloat16)
            return carry

        lax.fori_loop(0, rows_out // 16, group, 0)


def tables(zonal, meridional, codes, place, nx, ny, width):
    levels = zonal.shape[0]
    lon = lax.rem(
        place * width - HALO + nx + jnp.arange(width + 2 * HALO, dtype=jnp.int32), nx
    )
    lat = jnp.arange(ny, dtype=jnp.int32)
    lon_phase = (lon[None, :, None] * zonal[:, None, :] % nx).astype(jnp.float32) * (
        2.0 * math.pi / nx
    )
    lat_phase = (meridional[:, :, None] * lat[None, None, :] % ny).astype(jnp.float32) * (
        2.0 * math.pi / ny
    )
    weights = (AMP_UNIT * codes.astype(jnp.float32))[:, None, :]
    left = jnp.concatenate([weights * jnp.cos(lon_phase), -weights * jnp.sin(lon_phase)], axis=2)
    right = jnp.concatenate([jnp.cos(lat_phase), jnp.sin(lat_phase)], axis=1)
    eye = jnp.eye(levels, dtype=jnp.float32)
    left = left[:, :, None, :] * eye[:, None, :, None]
    return left.reshape(-1, levels * left.shape[-1]), right.reshape(-1, ny)


def solution(mesh):
    n = mesh.shape["gx"]
    members = mesh.shape["member"]

    def shards(analysis, zonal, meridional, codes):
        comps, levels, own, nx = analysis.shape
        ny = n * own
        width = nx // n
        wide = width + 2 * HALO
        half = ceil_to(own // 2, 16)
        place = lax.axis_index("gx")
        left, right = tables(zonal, meridional, codes, place, nx, ny, width)
        lat = (math.pi / 3.0) * (2.0 * (np.arange(ny) + 0.5) / ny - 1.0)
        geo = np.stack([1.0 / np.cos(lat), TIME_STEP * 2.0 * np.sin(lat)]).astype(np.float32)
        mats = []
        for step in range(STEPS):
            mats += [jnp.asarray(m, jnp.bfloat16) for m in stencils(levels, wide - 4 * step)]
        received = gather(analysis, n, members)
        rows_in = levels * wide
        rows_out = rows_in - 4 * levels
        pad = ny + LANES
        vmem = pl.BlockSpec(memory_space=pltpu.VMEM)
        out = pl.pallas_call(
            functools.partial(steps_kernel, (n, comps, levels, own, half, width)),
            out_shape=jax.ShapeDtypeStruct((comps, levels * width, ny), jnp.bfloat16),
            in_specs=[vmem] * (5 + 3 * STEPS),
            out_specs=vmem,
            scratch_shapes=[
                pltpu.VMEM((comps, rows_in, ny), jnp.bfloat16),
                pltpu.VMEM((2 * rows_in, ny), jnp.bfloat16),
                pltpu.VMEM((3 * rows_out, pad), jnp.float32),
                pltpu.VMEM((3 * rows_out, pad), jnp.float32),
                pltpu.VMEM((4 * rows_out, pad), jnp.float32),
                pltpu.VMEM((rows_out, ny), jnp.float32),
            ],
            compiler_params=pltpu.CompilerParams(vmem_limit_bytes=48 * 2**20),
        )(
            received,
            jnp.asarray(placing(levels, width), jnp.bfloat16),
            left,
            right,
            jnp.asarray(geo),
            *mats,
        )
        return out.reshape(comps, levels, width, ny)

    placed = (P(None, None, "gx", None), P("member", None), P("member", None), P("member", None))
    return jax.shard_map(
        shards, mesh=mesh, in_specs=placed, out_specs=P("member", None, "gx", None), check_vma=False
    )
```

profile of v0, /device:TPU:26, one launch (start us, length us, event | category | flops | bytes accessed | tf_op | source)
XLA Modules:
  0.0 77.0 jit_solution(2463530042446034303)
XLA Ops:
  0.0 0.7 convert_multiply_fusion
  0.7 0.1 copy.19
  0.8 0.1 copy.21
  0.9 0.8 copy.20
  1.6 0.3 cosine_multiply_fusion
  2.0 0.1 broadcast_multiply_fusion
  2.1 0.2 mul.95
  2.3 0.1 copy.22.left_ref
  2.4 1.7 %fusion.5 = (f32[4,16,1536]{2,1,0:T(8,128)S(1)}, f32[4,16,1536]{2,1,0:T(8,128)S(1)}) fusion(s32[4,16]{1,0:T(4,128)S(1)} %copy-done.15), kind=kLoop, calls=%fused_computation.8 | loop fusion | flops 884736 | bytes 786688 | tf_op jit(solution)/shard_map/cos | solution.py:308
  4.1 0.1 pad_maximum_fusion
  4.1 0.0 copy-start.1
  4.1 0.0 copy-start.2
  4.2 0.0 copy-start.3
  4.2 0.0 copy-start.4
  4.2 0.0 copy-start.6
  4.2 0.0 copy-start.7
  4.2 0.0 copy-start.8
  4.2 0.0 copy-start.9
  4.2 0.0 copy-start.10
  4.3 0.0 copy-start.11
  4.3 0.0 copy-start.13
  4.3 0.0 copy-start.14
  4.3 40.1 %shard_map.172.r_ref = bf16[16,432,128]{2,1,0:T(8,128)(2,1)S(1)} custom-call(bf16[3,4,96,512]{3,2,1,0:T(8,128)(2,1)S(1)} %copy-done), custom_call_target="tpu_custom_call" | custom-call | tf_op jit(solution)/shard_map/pallas_call | solution.py:122
  44.6 32.4 %shard_map.173 = bf16[3,128,1536]{2,1,0:T(8,128)(2,1)} custom-call(bf16[16,432,128]{2,1,0:T(8,128)(2,1)S(1)} %shard_map.172.r_ref, bf16[192,256]{1,0:T(8,128)(2,1)S(1)} %copy-done.12, f32[192,128]{1,0:T(8,128)S(1)} %copy.22.left_ref, f32[128,1536]{1,0:T(8,128)S(1)} %bitcast.4, f32[2,1536]{1,0:T(2,128)S(1)} %copy-done.14, bf16[528,192]{1,0:T(8,128)(2,1)S(1)} %copy-done.4, ...), custom_call_target="tpu_custom_call" | custom-call | tf_op jit(solution)/shard_map/pallas_call | solution.py:336
  (23 shorter events, 0.1 us)
Async XLA Ops:
  0.0 2.4 %copy-start.15 = (s32[4,16]{1,0:T(4,128)S(1)}, s32[4,16]{1,0:T(4,128)}, u32[]{:S(2)}) copy-start(s32[4,16]{1,0:T(4,128)} %param.20) | copy-start | bytes 772
  2.4 1.7 %copy-start = (bf16[3,4,96,512]{3,2,1,0:T(8,128)(2,1)S(1)}, bf16[3,4,96,512]{3,2,1,0:T(8,128)(2,1)}, u32[]{:S(2)}) copy-start(bf16[3,4,96,512]{3,2,1,0:T(8,128)(2,1)} %x_ref.1) | copy-start | bytes 3538948
  4.1 40.3 %copy-start.1 = (bf16[704,192]{1,0:T(8,128)(2,1)S(1)}, bf16[704,192]{1,0:T(8,128)(2,1)}, u32[]{:S(2)}) copy-start(bf16[704,192]{1,0:T(8,128)(2,1)} %constant.74.clone.refs_1_) | copy-start | bytes 811012
  4.1 40.3 %copy-start.2 = (bf16[640,176]{1,0:T(8,128)(2,1)S(1)}, bf16[640,176]{1,0:T(8,128)(2,1)}, u32[]{:S(2)}) copy-start(bf16[640,176]{1,0:T(8,128)(2,1)} %constant.77.clone.refs_4_) | copy-start | bytes 675844
  4.2 40.3 %copy-start.3 = (bf16[576,160]{1,0:T(8,128)(2,1)S(1)}, bf16[576,160]{1,0:T(8,128)(2,1)}, u32[]{:S(2)}) copy-start(bf16[576,160]{1,0:T(8,128)(2,1)} %constant.80.clone.refs_7_) | copy-start | bytes 552964
  4.2 40.3 %copy-start.4 = (bf16[528,192]{1,0:T(8,128)(2,1)S(1)}, bf16[528,192]{1,0:T(8,128)(2,1)}, u32[]{:S(2)}) copy-start(bf16[528,192]{1,0:T(8,128)(2,1)} %constant.73.clone.refs_0_) | copy-start | bytes 608260
  4.2 40.3 %copy-start.5 = (bf16[512,144]{1,0:T(8,128)(2,1)S(1)}, bf16[512,144]{1,0:T(8,128)(2,1)}, u32[]{:S(2)}) copy-start(bf16[512,144]{1,0:T(8,128)(2,1)} %constant.83.clone.refs_10_) | copy-start | bytes 442372
  4.2 40.3 %copy-start.6 = (bf16[480,176]{1,0:T(8,128)(2,1)S(1)}, bf16[480,176]{1,0:T(8,128)(2,1)}, u32[]{:S(2)}) copy-start(bf16[480,176]{1,0:T(8,128)(2,1)} %constant.76.clone.refs_3_) | copy-start | bytes 506884
  4.2 40.3 %copy-start.7 = (bf16[432,160]{1,0:T(8,128)(2,1)S(1)}, bf16[432,160]{1,0:T(8,128)(2,1)}, u32[]{:S(2)}) copy-start(bf16[432,160]{1,0:T(8,128)(2,1)} %constant.79.clone.refs_6_) | copy-start | bytes 414724
  4.2 40.3 %copy-start.8 = (bf16[384,144]{1,0:T(8,128)(2,1)S(1)}, bf16[384,144]{1,0:T(8,128)(2,1)}, u32[]{:S(2)}) copy-start(bf16[384,144]{1,0:T(8,128)(2,1)} %constant.82.clone.refs_9_) | copy-start | bytes 331780
  4.2 40.3 %copy-start.9 = (bf16[176,384]{1,0:T(8,128)(2,1)S(1)}, bf16[176,384]{1,0:T(8,128)(2,1)}, u32[]{:S(2)}) copy-start(bf16[176,384]{1,0:T(8,128)(2,1)} %constant.75.clone.refs_2_) | copy-start | bytes 405508
  4.2 40.3 %copy-start.10 = (bf16[160,352]{1,0:T(8,128)(2,1)S(1)}, bf16[160,352]{1,0:T(8,128)(2,1)}, u32[]{:S(2)}) copy-start(bf16[160,352]{1,0:T(8,128)(2,1)} %constant.78.clone.refs_5_) | copy-start | bytes 337924
  4.3 40.3 %copy-start.11 = (bf16[144,320]{1,0:T(8,128)(2,1)S(1)}, bf16[144,320]{1,0:T(8,128)(2,1)}, u32[]{:S(2)}) copy-start(bf16[144,320]{1,0:T(8,128)(2,1)} %constant.81.clone.refs_8_) | copy-start | bytes 276484
  4.3 40.3 %copy-start.12 = (bf16[192,256]{1,0:T(8,128)(2,1)S(1)}, bf16[192,256]{1,0:T(8,128)(2,1)}, u32[]{:S(2)}) copy-start(bf16[192,256]{1,0:T(8,128)(2,1)} %constant.85.clone.place_ref) | copy-start | bytes 294916
  4.3 40.3 %copy-start.13 = (bf16[128,288]{1,0:T(8,128)(2,1)S(1)}, bf16[128,288]{1,0:T(8,128)(2,1)}, u32[]{:S(2)}) copy-start(bf16[128,288]{1,0:T(8,128)(2,1)} %constant.84.clone.refs_11_) | copy-start | bytes 221188
  4.3 40.3 %copy-start.14 = (f32[2,1536]{1,0:T(2,128)S(1)}, f32[2,1536]{1,0:T(2,128)}, u32[]{:S(2)}) copy-start(f32[2,1536]{1,0:T(2,128)} %constant.86.clone.geo_ref) | copy-start | bytes 36868
where the time goes:
time: 77.1 us; the launch traced here: 77 us
  Pallas kernels  72.5 us (94%)
  other arithmetic  2.87 us (4%)
  local copies, waits for them, and re-layouts  1.28 us (2%)
    pallas_call x1, Pallas kernels, gather(): pl.pallas_call(functools.partial(gather_kernel, n, members), out_shape=ja...  40.1 us
    pallas_call x1, Pallas kernels, shards(): pl.pallas_call(functools.partial(steps_kernel, (n, comps, levels, own, ha...  32.4 us
    cos x1, other arithmetic, tables(): right = jnp.concatenate([jnp.cos(lat_phase), jnp.sin(lat_phase)], axis=1)  1.65 us

commit v1 on v0

v1 whole, which is shorter than its diff:
```python
import functools
import math

import jax
import jax.numpy as jnp
import numpy as np
from jax import lax
from jax.experimental import pallas as pl
from jax.experimental.pallas import tpu as pltpu
from jax.sharding import PartitionSpec as P

STEPS = 4
HALO = 2 * STEPS
TIME_STEP = 0.15
FILTER = 0.03
AMP_UNIT = 0.04
LANES = 128
MESH = pl.DeviceIdType.MESH


def ceil_to(value, unit):
    return -(-value // unit) * unit


def turns(product, count):
    rest = product - jnp.floor(product * (1.0 / count)) * count
    return rest * (2.0 * math.pi / count)


def waves(me, n, own, nx, width, levels, lon_ref, lat_ref):
    ny = n * own
    wide = width + 2 * HALO
    shape = (levels * wide, lon_ref.shape[1])
    row = lax.broadcasted_iota(jnp.int32, shape, 0)
    lane = lax.broadcasted_iota(jnp.int32, shape, 1)
    level = jnp.zeros(shape, jnp.int32)
    for l in range(1, levels):
        level = level + jnp.where(row >= l * wide, 1, 0)
    lon = row - level * wide + (me * width - HALO)
    lon = jnp.where(lon < 0, lon + nx, jnp.where(lon >= nx, lon - nx, lon))
    phase = turns(lon.astype(jnp.float32) * lon_ref[0:1, :], float(nx))
    count = shape[1] // 2
    modes = count // levels
    sine = lane >= count
    within = lane - jnp.where(sine, count, 0)
    own_level = (within >= level * modes) & (within < level * modes + modes)
    left = jnp.where(sine, -jnp.sin(phase), jnp.cos(phase)) * lon_ref[1:2, :]
    left = jnp.where(own_level, left, 0.0)
    lat = lax.broadcasted_iota(jnp.int32, (count, ny), 1).astype(jnp.float32)
    phase = turns(lat * lat_ref[...], float(ny))
    right = jnp.concatenate([jnp.cos(phase), jnp.sin(phase)], axis=0)
    return jnp.dot(
        left, right, preferred_element_type=jnp.float32, precision=lax.Precision.HIGHEST
    )


def gather_kernel(n, x_ref, lon_ref, lat_ref, out_ref, added_ref, send_ref, send_sem, recv_sem, fsend_sem, frecv_sem):
    comps, levels, own, nx = x_ref.shape
    width = nx // n
    total = out_ref.shape[1]
    half = ceil_to(own // 2, 16)
    me = lax.axis_index("gx")
    member = lax.axis_index("member")
    parity = lax.rem(member, 2)
    partner = member + 1 - 2 * parity

    barrier = pltpu.get_barrier_semaphore()
    for off in range(1, n):
        pl.semaphore_signal(
            barrier, inc=1, device_id=(member, lax.rem(me + off, n)), device_id_type=MESH
        )
    pl.semaphore_signal(barrier, inc=1, device_id=(partner, me), device_id_type=MESH)

    cut = ceil_to(total // 2, 16)
    parts = (pl.ds(0, cut), pl.ds(cut, total - cut))
    group = LANES // width
    tiles = nx // LANES
    mine_tile = lax.div(me, group)

    def flipped(value, bits):
        result = value
        b = 1
        while b <= bits:
            if bits & b:
                result = result + b * (1 - 2 * lax.rem(lax.div(value, b), 2))
            b *= 2
        return result

    def tile_columns(c, tile):
        first = pl.multiple_of(tile * LANES, LANES)
        return [x_ref[c, l, :, pl.ds(first, LANES)] for l in range(levels)]

    def pack(tile):
        before = lax.rem(tile + tiles - 1, tiles)
        after = lax.rem(tile + 1, tiles)
        for c in range(comps):
            here = tile_columns(c, tile)
            low = [x[:, LANES - HALO :] for x in tile_columns(c, before)]
            high = [x[:, :HALO] for x in tile_columns(c, after)]
            for d in range(group):
                t = tile * group + d
                first = d * width
                last = first + width
                main = [x[:, first:last] for x in here]
                send_ref[t, c * own : (c + 1) * own, :] = jnp.concatenate(main, axis=1)
                edges = []
                for l in range(levels):
                    edges.append(here[l][:, first - HALO : first] if d else low[l])
                    edges.append(here[l][:, last : last + HALO] if last < LANES else high[l])
                edge = jnp.concatenate(edges, axis=1)
                packed = jnp.concatenate([edge[:half], edge[own - half :]], axis=1)
                start = comps * own + c * half
                send_ref[t, start : start + half, :] = packed

    def spread(flip, mine):
        target = flipped(me, flip)
        return pltpu.make_async_remote_copy(
            src_ref=send_ref.at[target, mine],
            dst_ref=out_ref.at[me, mine],
            send_sem=send_sem.at[flip],
            recv_sem=recv_sem.at[flip],
            device_id=(member, target),
            device_id_type=MESH,
        )

    def arrival(flip, mine):
        source = flipped(me, flip)
        return pltpu.make_async_remote_copy(
            src_ref=send_ref.at[source, mine],
            dst_ref=out_ref.at[source, mine],
            send_sem=send_sem.at[flip],
            recv_sem=recv_sem.at[flip],
            device_id=(member, source),
            device_id_type=MESH,
        )

    def forward(flip, rows):
        source = flipped(me, flip)
        return pltpu.make_async_remote_copy(
            src_ref=out_ref.at[source, rows],
            dst_ref=out_ref.at[source, rows],
            send_sem=fsend_sem.at[flip],
            recv_sem=frecv_sem.at[flip],
            device_id=(partner, me),
            device_id_type=MESH,
        )

    order = []
    for tile_flip in range(tiles - 1, -1, -1):
        pack(flipped(mine_tile, tile_flip))
        if tile_flip == tiles - 1:
            pl.semaphore_wait(barrier, n)
        flips = [tile_flip * group + d for d in range(group - 1, -1, -1)]
        flips = [f for f in flips if f]
        order += flips
        for p in range(2):

            @pl.when(parity == p)
            def _(p=p, flips=flips):
                for f in flips:
                    spread(f, parts[p]).start()

    out_ref[me] = send_ref[me]
    added_ref[...] = waves(me, n, own, nx, width, levels, lon_ref, lat_ref)

    def exchange(mine, other):
        for f in order:
            arrival(f, mine).wait_recv()
            forward(f, mine).start()
        for f in order:
            forward(f, other).wait_recv()
        for f in order:
            spread(f, mine).wait_send()
            forward(f, mine).wait_send()

    @pl.when(parity == 0)
    def _():
        exchange(parts[0], parts[1])

    @pl.when(parity == 1)
    def _():
        exchange(parts[1], parts[0])


def gather(analysis, zonal, meridional, codes, n):
    comps, levels, own, nx = analysis.shape
    half = ceil_to(own // 2, 16)
    total = comps * (own + half)
    width = nx // n
    zonal = zonal.astype(jnp.float32).reshape(1, -1)
    weights = AMP_UNIT * codes.astype(jnp.float32).reshape(1, -1)
    lon_waves = jnp.tile(jnp.concatenate([zonal, weights], axis=0), (1, 2))
    lat_waves = meridional.astype(jnp.float32).reshape(-1, 1)
    vmem = pl.BlockSpec(memory_space=pltpu.VMEM)
    return pl.pallas_call(
        functools.partial(gather_kernel, n),
        out_shape=(
            jax.ShapeDtypeStruct((n, total, LANES), jnp.bfloat16),
            jax.ShapeDtypeStruct((levels * (width + 2 * HALO), n * own), jnp.float32),
        ),
        in_specs=[vmem] * 3,
        out_specs=(vmem, vmem),
        scratch_shapes=[pltpu.VMEM((n, total, LANES), jnp.bfloat16)]
        + [pltpu.SemaphoreType.DMA((n,)) for _ in range(4)],
        compiler_params=pltpu.CompilerParams(
            collective_id=0, has_side_effects=True, vmem_limit_bytes=24 * 2**20
        ),
    )(analysis, lon_waves, lat_waves)


def placing(levels, width):
    wide = width + 2 * HALO
    table = np.zeros((levels * wide, 2 * LANES), np.float32)
    for l in range(levels):
        for x in range(wide):
            row = l * wide + x
            if HALO <= x < HALO + width:
                table[row, l * width + x - HALO] = 1.0
            else:
                e = x if x < HALO else x - width
                lane = l * 2 * HALO + e
                table[row, LANES + lane] = 1.0
                table[row, LANES + LANES // 2 + lane] = 1.0
    return table


def stencils(levels, wide):
    out = wide - 4
    one = {
        "mid": (0, 0, 1, 0, 0),
        "slope": (1, -8, 0, 8, -1),
        "smooth": (1, -4, 6, -4, 1),
    }
    mats = {}
    for name, taps in one.items():
        m = np.zeros((out, wide), np.float32)
        for x in range(out):
            m[x, x : x + 5] = taps
        mats[name] = m
    eye = np.eye(levels, dtype=np.float32)
    k = np.arange(levels)
    mix = 0.25 + 0.25 * (k[None, :] >= k[:, None]).astype(np.float32)
    mid, slope, smooth = (np.kron(eye, mats[s]) for s in ("mid", "slope", "smooth"))
    wind = np.concatenate([mid, slope, smooth])
    thick = np.concatenate([mid, np.kron(mix, mats["slope"]), smooth, np.kron(mix, mats["mid"])])
    return wind, thick, slope


def steps_kernel(dims, r_ref, place_ref, added_ref, geo_ref, *refs):
    n, comps, levels, own, half, width = dims
    mats = refs[: 3 * STEPS]
    out_ref = refs[3 * STEPS]
    state_ref, hu_ref, wu_ref, wv_ref, wh_ref, wf_ref = refs[3 * STEPS + 1 :]
    ny = n * own
    wide = width + 2 * HALO
    rows = levels * wide
    pad = wu_ref.shape[1]

    row_index = lax.broadcasted_iota(jnp.int32, (n, 2 * half, LANES), 1)
    lane_index = lax.broadcasted_iota(jnp.int32, (n, 2 * half, LANES), 2)
    keep = (row_index < half) == (lane_index < LANES // 2)
    for c in range(comps):
        main = r_ref[:, c * own : (c + 1) * own, :]
        start = comps * own + c * half
        edge = r_ref[:, start : start + half, :]
        both = jnp.concatenate([edge, edge], axis=1)
        both = jnp.where(keep, both, jnp.zeros_like(both))
        if 2 * half > own:
            both = jnp.concatenate(
                [both[:, : own - half], both[:, half:]], axis=1
            )
        block = jnp.concatenate([main, both], axis=2).reshape(ny, 2 * LANES)
        field = lax.dot_general(
            place_ref[...], block, (((1,), (1,)), ((), ())), preferred_element_type=jnp.float32
        )
        if c == 0:
            field = field + added_ref[...]
        state_ref[c, :rows, :] = field.astype(jnp.bfloat16)

    for ref in (wu_ref, wv_ref, wh_ref):
        ref[:, ny:] = jnp.zeros((ref.shape[0], pad - ny), jnp.bfloat16)

    for step in range(STEPS):
        rows_in = levels * (wide - 4 * step)
        rows_out = levels * (wide - 4 * step - 4)
        wind, thick, flux = mats[3 * step : 3 * step + 3]
        column = 1.0 + state_ref[0, :rows_in, :].astype(jnp.float32)
        hu_ref[:rows_in, :] = (column * state_ref[1, :rows_in, :].astype(jnp.float32)).astype(
            jnp.bfloat16
        )

        def times(m_ref, x, into):
            into[: m_ref.shape[0], :ny] = jnp.dot(
                m_ref[...], x, preferred_element_type=jnp.float32
            ).astype(jnp.bfloat16)

        times(wind, state_ref[1, :rows_in, :], wu_ref)
        times(wind, state_ref[2, :rows_in, :], wv_ref)
        times(thick, state_ref[0, :rows_in, :], wh_ref)
        times(flux, hu_ref[:rows_in, :], wf_ref)

        def group(g, carry, rows_out=rows_out, last=step == STEPS - 1):
            size = 16

            def part(ref, which, lanes=ny):
                first = pl.multiple_of(which * rows_out + g * size, size)
                return ref[pl.ds(first, size), :lanes]

            def around(x):
                return [pltpu.roll(x, s % pad, 1) for s in (2, 1, -1, -2)]

            def slope(near):
                return (8.0 * (near[2] - near[1]) - (near[3] - near[0]))[:, :ny]

            def fourth(x, near):
                return ((near[0] + near[3]) - 4.0 * (near[1] + near[2]) + 6.0 * x)[:, :ny]

            inv = jnp.broadcast_to(geo_ref[0:1, :], (size, ny)).astype(jnp.bfloat16)
            cor = geo_ref[1:2, :]
            h, u, v, p = (
                part(wh_ref, 0, pad),
                part(wu_ref, 0, pad),
                part(wv_ref, 0, pad),
                part(wh_ref, 3, pad),
            )
            ha, ua, va = around(h), around(u), around(v)
            flux_y = slope([a + a * b for a, b in zip(va, ha)])
            press_y = slope(around(p))
            h_s, u_s, v_s = fourth(h, ha), fourth(u, ua), fourth(v, va)
            u_y, v_y = slope(ua), slope(va)
            h, u, v = h[:, :ny], u[:, :ny], v[:, :ny]
            u_x, v_x = part(wu_ref, 1), part(wv_ref, 1)
            ur = u * inv
            k = TIME_STEP / 12.0
            wide_type = jnp.float32
            h_t = inv * part(wf_ref, 0) + flux_y
            u_t = ur * u_x + v * u_y + inv * part(wh_ref, 1)
            v_t = ur * v_x + v * v_y + press_y
            h_s = h_s + part(wh_ref, 2)
            u_s = u_s + part(wu_ref, 2)
            v_s = v_s + part(wv_ref, 2)
            h, u, v, h_t, u_t, v_t, h_s, u_s, v_s = (
                x.astype(wide_type) for x in (h, u, v, h_t, u_t, v_t, h_s, u_s, v_s)
            )
            new_h = h - k * h_t - FILTER * h_s
            new_u = u - k * u_t + cor * v - FILTER * u_s
            new_v = v - k * v_t - cor * u - FILTER * v_s
            here = pl.ds(pl.multiple_of(g * size, size), size)
            target = out_ref if last else state_ref
            for c, value in enumerate((new_h, new_u, new_v)):
                target[c, here, :] = value.astype(jnp.bfloat16)
            return carry

        lax.fori_loop(0, rows_out // 16, group, 0)


def solution(mesh):
    n = mesh.shape["gx"]

    def shards(analysis, zonal, meridional, codes):
        comps, levels, own, nx = analysis.shape
        ny = n * own
        width = nx // n
        wide = width + 2 * HALO
        half = ceil_to(own // 2, 16)
        lat = (math.pi / 3.0) * (2.0 * (np.arange(ny) + 0.5) / ny - 1.0)
        geo = np.stack([1.0 / np.cos(lat), TIME_STEP * 2.0 * np.sin(lat)]).astype(np.float32)
        mats = []
        for step in range(STEPS):
            mats += [jnp.asarray(m, jnp.bfloat16) for m in stencils(levels, wide - 4 * step)]
        received, added = gather(analysis, zonal, meridional, codes, n)
        rows_in = levels * wide
        rows_out = rows_in - 4 * levels
        pad = ny + LANES
        vmem = pl.BlockSpec(memory_space=pltpu.VMEM)
        out = pl.pallas_call(
            functools.partial(steps_kernel, (n, comps, levels, own, half, width)),
            out_shape=jax.ShapeDtypeStruct((comps, levels * width, ny), jnp.bfloat16),
            in_specs=[vmem] * (4 + 3 * STEPS),
            out_specs=vmem,
            scratch_shapes=[
                pltpu.VMEM((comps, rows_in, ny), jnp.bfloat16),
                pltpu.VMEM((rows_in, ny), jnp.bfloat16),
                pltpu.VMEM((3 * rows_out, pad), jnp.bfloat16),
                pltpu.VMEM((3 * rows_out, pad), jnp.bfloat16),
                pltpu.VMEM((4 * rows_out, pad), jnp.bfloat16),
                pltpu.VMEM((rows_out, ny), jnp.bfloat16),
            ],
            compiler_params=pltpu.CompilerParams(vmem_limit_bytes=48 * 2**20),
        )(
            received,
            jnp.asarray(placing(levels, width), jnp.bfloat16),
            added,
            jnp.asarray(geo),
            *mats,
        )
        return out.reshape(comps, levels, width, ny)

    placed = (P(None, None, "gx", None), P("member", None), P("member", None), P("member", None))
    return jax.shard_map(
        shards, mesh=mesh, in_specs=placed, out_specs=P("member", None, "gx", None), check_vma=False
    )
```

time: 77.1 us -> 72.1 us (0.935)
  the two profiles are of different devices: /device:TPU:26 before, /device:TPU:0 now
where the time goes in v1:
time: 72.1 us; the launch traced here: 71.6 us
  Pallas kernels  60.5 us (84%)
  local copies, waits for them, and re-layouts  8.91 us (12%)
  other arithmetic  2.1 us (3%)
    pallas_call x1, Pallas kernels, gather(): pl.pallas_call(functools.partial(gather_kernel, n), out_shape=(jax.ShapeD...  38.8 us
    pallas_call x1, Pallas kernels, shards(): pl.pallas_call(functools.partial(steps_kernel, (n, comps, levels, own, ha...  21.7 us
    unnamed x30, local copies, waits for them, and re-layouts  8.57 us

profile of v1, /device:TPU:0, one launch (start us, length us, event | category | flops | bytes accessed | tf_op | source)
XLA Modules:
  0.0 71.6 jit_solution(1003515346956039002)
XLA Ops:
  0.0 0.7 convert_element_type.9
  0.7 0.1 reshape.28
  0.8 0.7 convert_element_type.11
  1.5 0.7 convert_multiply_fusion
  2.2 0.1 mul.19
  2.3 0.1 tile.10.lon_ref
  2.4 0.1 reshape.31.lat_ref
  2.5 0.0 copy-start
  2.5 1.3 %copy-done = bf16[3,4,96,512]{3,2,1,0:T(8,128)(2,1)S(1)} copy-done((bf16[3,4,96,512]{3,2,1,0:T(8,128)(2,1)S(1)}, bf16[3,4,96,512]{3,2,1,0:T(8,128)(2,1)}, u32[]{:S(2)}) %copy-start) | copy-done | bytes 1179672
  3.7 0.0 copy-start.14
  3.8 38.8 %shard_map.172 = (bf16[16,432,128]{2,1,0:T(8,128)(2,1)S(1)}, f32[192,1536]{1,0:T(8,128)S(1)}) custom-call(bf16[3,4,96,512]{3,2,1,0:T(8,128)(2,1)S(1)} %copy-done, f32[2,128]{1,0:T(2,128)S(1)} %tile.10.lon_ref, f32[64,1]{1,0:T(8,128)S(1)} %reshape.31.lat_ref), custom_call_target="tpu_custom_call" | custom-call | tf_op jit(solution)/shard_map/pallas_call | solution.py:195
  42.6 0.0 copy-done.12
  42.6 0.0 copy-done.1
  42.6 0.0 copy-done.2
  42.6 0.0 copy-start.4
  42.7 0.9 %copy-done.4 = bf16[528,192]{1,0:T(8,128)(2,1)S(1)} copy-done((bf16[528,192]{1,0:T(8,128)(2,1)S(1)}, bf16[528,192]{1,0:T(8,128)(2,1)}, u32[]{:S(2)}) %copy-start.4) | copy-done | bytes 202776
  43.6 0.9 %copy-done.5 = bf16[512,144]{1,0:T(8,128)(2,1)S(1)} copy-done((bf16[512,144]{1,0:T(8,128)(2,1)S(1)}, bf16[512,144]{1,0:T(8,128)(2,1)}, u32[]{:S(2)}) %copy-start.5) | copy-done | bytes 147480
  44.6 0.9 %copy-done.6 = bf16[480,176]{1,0:T(8,128)(2,1)S(1)} copy-done((bf16[480,176]{1,0:T(8,128)(2,1)S(1)}, bf16[480,176]{1,0:T(8,128)(2,1)}, u32[]{:S(2)}) %copy-start.6) | copy-done | bytes 168984
  45.5 0.9 %copy-done.8 = bf16[384,144]{1,0:T(8,128)(2,1)S(1)} copy-done((bf16[384,144]{1,0:T(8,128)(2,1)S(1)}, bf16[384,144]{1,0:T(8,128)(2,1)}, u32[]{:S(2)}) %copy-start.8) | copy-done | bytes 110616
  46.4 0.9 %copy-done.9 = bf16[192,256]{1,0:T(8,128)(2,1)S(1)} copy-done((bf16[192,256]{1,0:T(8,128)(2,1)S(1)}, bf16[192,256]{1,0:T(8,128)(2,1)}, u32[]{:S(2)}) %copy-start.9) | copy-done | bytes 98328
  47.3 0.9 %copy-done.10 = bf16[176,192]{1,0:T(8,128)(2,1)S(1)} copy-done((bf16[176,192]{1,0:T(8,128)(2,1)S(1)}, bf16[176,192]{1,0:T(8,128)(2,1)}, u32[]{:S(2)}) %copy-start.10) | copy-done | bytes 67608
  48.2 0.9 %copy-done.11 = bf16[160,176]{1,0:T(8,128)(2,1)S(1)} copy-done((bf16[160,176]{1,0:T(8,128)(2,1)S(1)}, bf16[160,176]{1,0:T(8,128)(2,1)}, u32[]{:S(2)}) %copy-start.11) | copy-done | bytes 56344
  49.1 0.8 %copy-done.13 = bf16[128,144]{1,0:T(8,128)(2,1)S(1)} copy-done((bf16[128,144]{1,0:T(8,128)(2,1)S(1)}, bf16[128,144]{1,0:T(8,128)(2,1)}, u32[]{:S(2)}) %copy-start.13) | copy-done | bytes 36888
  49.9 21.7 %shard_map.173 = bf16[3,128,1536]{2,1,0:T(8,128)(2,1)} custom-call(bf16[16,432,128]{2,1,0:T(8,128)(2,1)S(1)} %get-tuple-element.7.r_ref, bf16[192,256]{1,0:T(8,128)(2,1)S(1)} %copy-done.9, f32[192,1536]{1,0:T(8,128)S(1)} %get-tuple-element.8.added_ref, f32[2,1536]{1,0:T(2,128)S(1)} %copy-done.14, bf16[528,192]{1,0:T(8,128)(2,1)S(1)} %copy-done.4, ...), custom_call_target="tpu_custom_call" | custom-call | tf_op jit(solution)/shard_map/pallas_call | solution.py:376
  (17 shorter events, 0.0 us)
Async XLA Ops:
  0.0 42.6 %copy-start.12 = (bf16[144,160]{1,0:T(8,128)(2,1)S(1)}, bf16[144,160]{1,0:T(8,128)(2,1)}, u32[]{:S(2)}) copy-start(bf16[144,160]{1,0:T(8,128)(2,1)} %constant.38.clone.refs_8_) | copy-start | bytes 138244
  2.5 1.3 %copy-start = (bf16[3,4,96,512]{3,2,1,0:T(8,128)(2,1)S(1)}, bf16[3,4,96,512]{3,2,1,0:T(8,128)(2,1)}, u32[]{:S(2)}) copy-start(bf16[3,4,96,512]{3,2,1,0:T(8,128)(2,1)} %x_ref.1) | copy-start | bytes 3538948
  3.7 38.9 %copy-start.1 = (bf16[704,192]{1,0:T(8,128)(2,1)S(1)}, bf16[704,192]{1,0:T(8,128)(2,1)}, u32[]{:S(2)}) copy-start(bf16[704,192]{1,0:T(8,128)(2,1)} %constant.31.clone.refs_1_) | copy-start | bytes 811012
  3.7 38.9 %copy-start.2 = (bf16[640,176]{1,0:T(8,128)(2,1)S(1)}, bf16[640,176]{1,0:T(8,128)(2,1)}, u32[]{:S(2)}) copy-start(bf16[640,176]{1,0:T(8,128)(2,1)} %constant.34.clone.refs_4_) | copy-start | bytes 675844
  3.7 38.9 %copy-start.3 = (bf16[576,160]{1,0:T(8,128)(2,1)S(1)}, bf16[576,160]{1,0:T(8,128)(2,1)}, u32[]{:S(2)}) copy-start(bf16[576,160]{1,0:T(8,128)(2,1)} %constant.37.clone.refs_7_) | copy-start | bytes 552964
  3.7 38.9 %copy-start.7 = (bf16[432,160]{1,0:T(8,128)(2,1)S(1)}, bf16[432,160]{1,0:T(8,128)(2,1)}, u32[]{:S(2)}) copy-start(bf16[432,160]{1,0:T(8,128)(2,1)} %constant.36.clone.refs_6_) | copy-start | bytes 414724
  3.7 38.9 %copy-start.14 = (f32[2,1536]{1,0:T(2,128)S(1)}, f32[2,1536]{1,0:T(2,128)}, u32[]{:S(2)}) copy-start(f32[2,1536]{1,0:T(2,128)} %constant.43.clone.geo_ref) | copy-start | bytes 36868
  42.6 1.0 %copy-start.4 = (bf16[528,192]{1,0:T(8,128)(2,1)S(1)}, bf16[528,192]{1,0:T(8,128)(2,1)}, u32[]{:S(2)}) copy-start(bf16[528,192]{1,0:T(8,128)(2,1)} %constant.30.clone.refs_0_) | copy-start | bytes 608260
  43.6 0.9 %copy-start.5 = (bf16[512,144]{1,0:T(8,128)(2,1)S(1)}, bf16[512,144]{1,0:T(8,128)(2,1)}, u32[]{:S(2)}) copy-start(bf16[512,144]{1,0:T(8,128)(2,1)} %constant.40.clone.refs_10_) | copy-start | bytes 442372
  44.5 0.9 %copy-start.6 = (bf16[480,176]{1,0:T(8,128)(2,1)S(1)}, bf16[480,176]{1,0:T(8,128)(2,1)}, u32[]{:S(2)}) copy-start(bf16[480,176]{1,0:T(8,128)(2,1)} %constant.33.clone.refs_3_) | copy-start | bytes 506884
  45.5 0.9 %copy-start.8 = (bf16[384,144]{1,0:T(8,128)(2,1)S(1)}, bf16[384,144]{1,0:T(8,128)(2,1)}, u32[]{:S(2)}) copy-start(bf16[384,144]{1,0:T(8,128)(2,1)} %constant.39.clone.refs_9_) | copy-start | bytes 331780
  46.4 0.9 %copy-start.9 = (bf16[192,256]{1,0:T(8,128)(2,1)S(1)}, bf16[192,256]{1,0:T(8,128)(2,1)}, u32[]{:S(2)}) copy-start(bf16[192,256]{1,0:T(8,128)(2,1)} %constant.42.clone.place_ref) | copy-start | bytes 294916
  47.3 0.9 %copy-start.10 = (bf16[176,192]{1,0:T(8,128)(2,1)S(1)}, bf16[176,192]{1,0:T(8,128)(2,1)}, u32[]{:S(2)}) copy-start(bf16[176,192]{1,0:T(8,128)(2,1)} %constant.32.clone.refs_2_) | copy-start | bytes 202756
  48.2 0.9 %copy-start.11 = (bf16[160,176]{1,0:T(8,128)(2,1)S(1)}, bf16[160,176]{1,0:T(8,128)(2,1)}, u32[]{:S(2)}) copy-start(bf16[160,176]{1,0:T(8,128)(2,1)} %constant.35.clone.refs_5_) | copy-start | bytes 168964
  49.1 0.8 %copy-start.13 = (bf16[128,144]{1,0:T(8,128)(2,1)S(1)}, bf16[128,144]{1,0:T(8,128)(2,1)}, u32[]{:S(2)}) copy-start(bf16[128,144]{1,0:T(8,128)(2,1)} %constant.41.clone.refs_11_) | copy-start | bytes 110596

commit v2 on v1

--- a/solution.py
+++ b/solution.py
@@ -3,7 +3,6 @@
 
 import jax
 import jax.numpy as jnp
-import numpy as np
 from jax import lax
 from jax.experimental import pallas as pl
 from jax.experimental.pallas import tpu as pltpu
@@ -27,10 +26,25 @@
     return rest * (2.0 * math.pi / count)
 
 
-def waves(me, n, own, nx, width, levels, lon_ref, lat_ref):
+def waves(me, n, own, nx, width, levels, zonal, meridional, codes):
+    def in_row(x):
+        x = x.astype(jnp.float32)
+        return jnp.concatenate([x[l : l + 1, :] for l in range(levels)], axis=1)
+
+    zonal, meridional, codes = in_row(zonal), in_row(meridional), in_row(codes)
+    count = zonal.shape[1]
+    square = (count, count)
+    diagonal = lax.broadcasted_iota(jnp.int32, square, 0) == lax.broadcasted_iota(
+        jnp.int32, square, 1
+    )
+    meridional = jnp.sum(
+        jnp.where(diagonal, jnp.broadcast_to(meridional, square), 0.0), axis=1, keepdims=True
+    )
+    zonal = jnp.concatenate([zonal, zonal], axis=1)
+    weights = AMP_UNIT * jnp.concatenate([codes, codes], axis=1)
     ny = n * own
     wide = width + 2 * HALO
-    shape = (levels * wide, lon_ref.shape[1])
+    shape = (levels * wide, 2 * count)
     row = lax.broadcasted_iota(jnp.int32, shape, 0)
     lane = lax.broadcasted_iota(jnp.int32, shape, 1)
     level = jnp.zeros(shape, jnp.int32)
@@ -38,23 +52,38 @@
         level = level + jnp.where(row >= l * wide, 1, 0)
     lon = row - level * wide + (me * width - HALO)
     lon = jnp.where(lon < 0, lon + nx, jnp.where(lon >= nx, lon - nx, lon))
-    phase = turns(lon.astype(jnp.float32) * lon_ref[0:1, :], float(nx))
-    count = shape[1] // 2
+    phase = turns(lon.astype(jnp.float32) * zonal, float(nx))
     modes = count // levels
     sine = lane >= count
     within = lane - jnp.where(sine, count, 0)
     own_level = (within >= level * modes) & (within < level * modes + modes)
-    left = jnp.where(sine, -jnp.sin(phase), jnp.cos(phase)) * lon_ref[1:2, :]
+    left = jnp.where(sine, -jnp.sin(phase), jnp.cos(phase)) * weights
     left = jnp.where(own_level, left, 0.0)
     lat = lax.broadcasted_iota(jnp.int32, (count, ny), 1).astype(jnp.float32)
-    phase = turns(lat * lat_ref[...], float(ny))
+    phase = turns(lat * meridional, float(ny))
     right = jnp.concatenate([jnp.cos(phase), jnp.sin(phase)], axis=0)
     return jnp.dot(
         left, right, preferred_element_type=jnp.float32, precision=lax.Precision.HIGHEST
     )
 
 
-def gather_kernel(n, x_ref, lon_ref, lat_ref, out_ref, added_ref, send_ref, send_sem, recv_sem, fsend_sem, frecv_sem):
+def gather_kernel(
+    n,
+    x_ref,
+    zonal_ref,
+    meridional_ref,
+    codes_ref,
+    out_ref,
+    added_ref,
+    mats_ref,
+    place_ref,
+    geo_ref,
+    send_ref,
+    send_sem,
+    recv_sem,
+    fsend_sem,
+    frecv_sem,
+):
     comps, levels, own, nx = x_ref.shape
     width = nx // n
     total = out_ref.shape[1]
@@ -160,11 +189,34 @@
                 for f in flips:
                     spread(f, parts[p]).start()
 
+    near = [f for f in order if f < n // 2][::-1]
+    far = [f for f in order if f >= n // 2]
+
+    def early(mine):
+        for f in near[: group - 1]:
+            arrival(f, mine).wait_recv()
+            forward(f, mine).start()
+
+    for p in range(2):
+        pl.when(parity == p)(functools.partial(early, parts[p]))
     out_ref[me] = send_ref[me]
-    added_ref[...] = waves(me, n, own, nx, width, levels, lon_ref, lat_ref)
+    place_ref[...] = placing(levels, width)
+    geo_ref[...] = geometry(n * own)
+    base = 0
+    for step in range(STEPS):
+        for block in stencils(levels, width + 2 * HALO - 4 * step):
+            mats_ref[base : base + block.shape[0], : block.shape[1]] = block
+            base += block.shape[0]
+    added_ref[...] = waves(
+        me, n, own, nx, width, levels, zonal_ref[...], meridional_ref[...], codes_ref[...]
+    )
 
     def exchange(mine, other):
-        for f in order:
+        pending = near[group - 1 :]
+        for i, f in enumerate(far):
+            if i < len(pending):
+                arrival(pending[i], mine).wait_recv()
+                forward(pending[i], mine).start()
             arrival(f, mine).wait_recv()
             forward(f, mine).start()
         for f in order:
@@ -187,70 +239,80 @@
     half = ceil_to(own // 2, 16)
     total = comps * (own + half)
     width = nx // n
-    zonal = zonal.astype(jnp.float32).reshape(1, -1)
-    weights = AMP_UNIT * codes.astype(jnp.float32).reshape(1, -1)
-    lon_waves = jnp.tile(jnp.concatenate([zonal, weights], axis=0), (1, 2))
-    lat_waves = meridional.astype(jnp.float32).reshape(-1, 1)
+    rows = levels * (width + 2 * HALO)
+    mat_rows = sum(5 * (rows - 4 * levels * (step + 1)) for step in range(STEPS))
     vmem = pl.BlockSpec(memory_space=pltpu.VMEM)
     return pl.pallas_call(
         functools.partial(gather_kernel, n),
         out_shape=(
             jax.ShapeDtypeStruct((n, total, LANES), jnp.bfloat16),
-            jax.ShapeDtypeStruct((levels * (width + 2 * HALO), n * own), jnp.float32),
+            jax.ShapeDtypeStruct((rows, n * own), jnp.float32),
+            jax.ShapeDtypeStruct((mat_rows, rows), jnp.bfloat16),
+            jax.ShapeDtypeStruct((rows, 2 * LANES), jnp.bfloat16),
+            jax.ShapeDtypeStruct((2, n * own), jnp.float32),
         ),
-        in_specs=[vmem] * 3,
-        out_specs=(vmem, vmem),
+        in_specs=[vmem] * 4,
+        out_specs=(vmem,) * 5,
         scratch_shapes=[pltpu.VMEM((n, total, LANES), jnp.bfloat16)]
         + [pltpu.SemaphoreType.DMA((n,)) for _ in range(4)],
         compiler_params=pltpu.CompilerParams(
             collective_id=0, has_side_effects=True, vmem_limit_bytes=24 * 2**20
         ),
-    )(analysis, lon_waves, lat_waves)
+    )(analysis, zonal, meridional, codes)
+
+
+def level_and_column(shape, axis, levels, wide):
+    index = lax.broadcasted_iota(jnp.int32, shape, axis)
+    level = jnp.zeros(shape, jnp.int32)
+    for l in range(1, levels):
+        level = level + jnp.where(index >= l * wide, 1, 0)
+    return level, index - level * wide
 
 
 def placing(levels, width):
     wide = width + 2 * HALO
-    table = np.zeros((levels * wide, 2 * LANES), np.float32)
-    for l in range(levels):
-        for x in range(wide):
-            row = l * wide + x
-            if HALO <= x < HALO + width:
-                table[row, l * width + x - HALO] = 1.0
-            else:
-                e = x if x < HALO else x - width
-                lane = l * 2 * HALO + e
-                table[row, LANES + lane] = 1.0
-                table[row, LANES + LANES // 2 + lane] = 1.0
-    return table
+    shape = (levels * wide, 2 * LANES)
+    level, x = level_and_column(shape, 0, levels, wide)
+    lane = lax.broadcasted_iota(jnp.int32, shape, 1)
+    inside = (x >= HALO) & (x < HALO + width)
+    main = level * width + x - HALO
+    edge = LANES + level * 2 * HALO + jnp.where(x < HALO, x, x - width)
+    hit = (lane == jnp.where(inside, main, edge)) | (
+        jnp.logical_not(inside) & (lane == edge + LANES // 2)
+    )
+    return jnp.where(hit, 1.0, 0.0).astype(jnp.bfloat16)
 
 
 def stencils(levels, wide):
     out = wide - 4
-    one = {
-        "mid": (0, 0, 1, 0, 0),
-        "slope": (1, -8, 0, 8, -1),
-        "smooth": (1, -4, 6, -4, 1),
-    }
-    mats = {}
-    for name, taps in one.items():
-        m = np.zeros((out, wide), np.float32)
-        for x in range(out):
-            m[x, x : x + 5] = taps
-        mats[name] = m
-    eye = np.eye(levels, dtype=np.float32)
-    k = np.arange(levels)
-    mix = 0.25 + 0.25 * (k[None, :] >= k[:, None]).astype(np.float32)
-    mid, slope, smooth = (np.kron(eye, mats[s]) for s in ("mid", "slope", "smooth"))
-    wind = np.concatenate([mid, slope, smooth])
-    thick = np.concatenate([mid, np.kron(mix, mats["slope"]), smooth, np.kron(mix, mats["mid"])])
-    return wind, thick, slope
-
-
-def steps_kernel(dims, r_ref, place_ref, added_ref, geo_ref, *refs):
+    shape = (levels * out, levels * wide)
+    level, x = level_and_column(shape, 0, levels, out)
+    from_level, from_x = level_and_column(shape, 1, levels, wide)
+    step = from_x - x
+
+    def taps(*values):
+        result = jnp.zeros(shape, jnp.float32)
+        for i, value in enumerate(values):
+            if value:
+                result = jnp.where(step == i, float(value), result)
+        return result
+
+    same = jnp.where(level == from_level, 1.0, 0.0)
+    mix = jnp.where(from_level >= level, 0.5, 0.25)
+    slope, mid, smooth = taps(1, -8, 0, 8, -1), taps(0, 0, 1), taps(1, -4, 6, -4, 1)
+    blocks = (slope * same, mid * same, smooth * same, slope * mix, mid * mix)
+    return [b.astype(jnp.bfloat16) for b in blocks]
+
+
+def geometry(ny):
+    lat = lax.broadcasted_iota(jnp.int32, (1, ny), 1).astype(jnp.float32)
+    lat = (math.pi / 3.0) * (2.0 * (lat + 0.5) / ny - 1.0)
+    return jnp.concatenate([1.0 / jnp.cos(lat), (2.0 * TIME_STEP) * jnp.sin(lat)], axis=0)
+
+
+def steps_kernel(dims, r_ref, added_ref, mats_ref, place_ref, geo_ref, out_ref, *refs):
     n, comps, levels, own, half, width = dims
-    mats = refs[: 3 * STEPS]
-    out_ref = refs[3 * STEPS]
-    state_ref, hu_ref, wu_ref, wv_ref, wh_ref, wf_ref = refs[3 * STEPS + 1 :]
+    state_ref, hu_ref, wu_ref, wv_ref, wh_ref, wf_ref = refs
     ny = n * own
     wide = width + 2 * HALO
     rows = levels * wide
@@ -280,18 +342,23 @@
     for ref in (wu_ref, wv_ref, wh_ref):
         ref[:, ny:] = jnp.zeros((ref.shape[0], pad - ny), jnp.bfloat16)
 
+    base = 0
     for step in range(STEPS):
         rows_in = levels * (wide - 4 * step)
         rows_out = levels * (wide - 4 * step - 4)
-        wind, thick, flux = mats[3 * step : 3 * step + 3]
+        slope_at, mid_at, last_at = base, base + rows_out, base + 5 * rows_out
+        wind = mats_ref[slope_at : slope_at + 3 * rows_out, :rows_in]
+        thick = mats_ref[mid_at:last_at, :rows_in]
+        flux = mats_ref[slope_at:mid_at, :rows_in]
+        base = last_at
         column = 1.0 + state_ref[0, :rows_in, :].astype(jnp.float32)
         hu_ref[:rows_in, :] = (column * state_ref[1, :rows_in, :].astype(jnp.float32)).astype(
             jnp.bfloat16
         )
 
-        def times(m_ref, x, into):
-            into[: m_ref.shape[0], :ny] = jnp.dot(
-                m_ref[...], x, preferred_element_type=jnp.float32
+        def times(matrix, x, into):
+            into[: matrix.shape[0], :ny] = jnp.dot(
+                matrix, x, preferred_element_type=jnp.float32
             ).astype(jnp.bfloat16)
 
         times(wind, state_ref[1, :rows_in, :], wu_ref)
@@ -319,8 +386,8 @@
             cor = geo_ref[1:2, :]
             h, u, v, p = (
                 part(wh_ref, 0, pad),
-                part(wu_ref, 0, pad),
-                part(wv_ref, 0, pad),
+                part(wu_ref, 1, pad),
+                part(wv_ref, 1, pad),
                 part(wh_ref, 3, pad),
             )
             ha, ua, va = around(h), around(u), around(v)
@@ -329,14 +396,14 @@
             h_s, u_s, v_s = fourth(h, ha), fourth(u, ua), fourth(v, va)
             u_y, v_y = slope(ua), slope(va)
             h, u, v = h[:, :ny], u[:, :ny], v[:, :ny]
-            u_x, v_x = part(wu_ref, 1), part(wv_ref, 1)
+            u_x, v_x = part(wu_ref, 0), part(wv_ref, 0)
             ur = u * inv
             k = TIME_STEP / 12.0
             wide_type = jnp.float32
             h_t = inv * part(wf_ref, 0) + flux_y
-            u_t = ur * u_x + v * u_y + inv * part(wh_ref, 1)
+            u_t = ur * u_x + v * u_y + inv * part(wh_ref, 2)
             v_t = ur * v_x + v * v_y + press_y
-            h_s = h_s + part(wh_ref, 2)
+            h_s = h_s + part(wh_ref, 1)
             u_s = u_s + part(wu_ref, 2)
             v_s = v_s + part(wv_ref, 2)
             h, u, v, h_t, u_t, v_t, h_s, u_s, v_s = (
@@ -363,12 +430,7 @@
         width = nx // n
         wide = width + 2 * HALO
         half = ceil_to(own // 2, 16)
-        lat = (math.pi / 3.0) * (2.0 * (np.arange(ny) + 0.5) / ny - 1.0)
-        geo = np.stack([1.0 / np.cos(lat), TIME_STEP * 2.0 * np.sin(lat)]).astype(np.float32)
-        mats = []
-        for step in range(STEPS):
-            mats += [jnp.asarray(m, jnp.bfloat16) for m in stencils(levels, wide - 4 * step)]
-        received, added = gather(analysis, zonal, meridional, codes, n)
+        gathered = gather(analysis, zonal, meridional, codes, n)
         rows_in = levels * wide
         rows_out = rows_in - 4 * levels
         pad = ny + LANES
@@ -376,7 +438,7 @@
         out = pl.pallas_call(
             functools.partial(steps_kernel, (n, comps, levels, own, half, width)),
             out_shape=jax.ShapeDtypeStruct((comps, levels * width, ny), jnp.bfloat16),
-            in_specs=[vmem] * (4 + 3 * STEPS),
+            in_specs=[vmem] * 5,
             out_specs=vmem,
             scratch_shapes=[
                 pltpu.VMEM((comps, rows_in, ny), jnp.bfloat16),
@@ -387,13 +449,7 @@
                 pltpu.VMEM((rows_out, ny), jnp.bfloat16),
             ],
             compiler_params=pltpu.CompilerParams(vmem_limit_bytes=48 * 2**20),
-        )(
-            received,
-            jnp.asarray(placing(levels, width), jnp.bfloat16),
-            added,
-            jnp.asarray(geo),
-            *mats,
-        )
+        )(*gathered)
         return out.reshape(comps, levels, width, ny)
 
     placed = (P(None, None, "gx", None), P("member", None), P("member", None), P("member", None))

time: 72.1 us -> 63.5 us (0.88)
  the two profiles are of different devices: /device:TPU:0 before, /device:TPU:10 now
where the time goes in v2:
time: 63.5 us; the launch traced here: 63.3 us
  Pallas kernels  60 us (94%)
  local copies, waits for them, and re-layouts  3.31 us (5%)
    pallas_call x1, Pallas kernels, gather(): pl.pallas_call(functools.partial(gather_kernel, n), out_shape=(jax.ShapeD...  38.3 us
    pallas_call x1, Pallas kernels, shards(): pl.pallas_call(functools.partial(steps_kernel, (n, comps, levels, own, ha...  21.6 us
    unnamed x8, local copies, waits for them, and re-layouts  3.31 us

profile of v2, /device:TPU:10, one launch (start us, length us, event | category | flops | bytes accessed | tf_op | source)
XLA Modules:
  0.0 63.3 jit_solution(18286219167576949037)
XLA Ops:
  0.0 0.0 copy-start
  0.0 1.3 %copy-done = bf16[3,4,96,512]{3,2,1,0:T(8,128)(2,1)S(1)} copy-done((bf16[3,4,96,512]{3,2,1,0:T(8,128)(2,1)S(1)}, bf16[3,4,96,512]{3,2,1,0:T(8,128)(2,1)}, u32[]{:S(2)}) %copy-start) | copy-done | bytes 1179672
  1.3 0.0 copy-start.1
  1.3 0.7 %copy-done.1 = s32[4,16]{1,0:T(4,128)S(1)} copy-done((s32[4,16]{1,0:T(4,128)S(1)}, s32[4,16]{1,0:T(4,128)}, u32[]{:S(2)}) %copy-start.1) | copy-done | bytes 280
  2.0 0.0 copy-start.2
  2.0 0.7 %copy-done.2 = s32[4,16]{1,0:T(4,128)S(1)} copy-done((s32[4,16]{1,0:T(4,128)S(1)}, s32[4,16]{1,0:T(4,128)}, u32[]{:S(2)}) %copy-start.2) | copy-done | bytes 280
  2.6 0.0 copy-start.3
  2.6 0.7 %copy-done.3 = s32[4,16]{1,0:T(4,128)S(1)} copy-done((s32[4,16]{1,0:T(4,128)S(1)}, s32[4,16]{1,0:T(4,128)}, u32[]{:S(2)}) %copy-start.3) | copy-done | bytes 280
  3.3 38.3 %shard_map.46 = (bf16[16,432,128]{2,1,0:T(8,128)(2,1)S(1)}, f32[192,1536]{1,0:T(8,128)S(1)}, bf16[3040,192]{1,0:T(8,128)(2,1)S(1)}, bf16[192,256]{1,0:T(8,128)(2,1)S(1)}, f32[2,1536]{1,0:T(2,128)S(1)}) custom-call(bf16[3,4,96,512]{3,2,1,0:T(8,128)(2,1)S(1)} %copy-done, s32[4,16]{1,0:T(4,128)S(1)} %copy-done.1, s32[4,16]{1,0:T(4,128)S(1)} %copy-done.2, ...), custom_call_target="tpu_custom_call" | custom-call | tf_op jit(solution)/shard_map/pallas_call | solution.py:245
  41.7 21.6 %shard_map.47 = bf16[3,128,1536]{2,1,0:T(8,128)(2,1)} custom-call(bf16[16,432,128]{2,1,0:T(8,128)(2,1)S(1)} %get-tuple-element.10.r_ref, f32[192,1536]{1,0:T(8,128)S(1)} %get-tuple-element.11.added_ref, bf16[3040,192]{1,0:T(8,128)(2,1)S(1)} %get-tuple-element.12.mats_ref, bf16[192,256]{1,0:T(8,128)(2,1)S(1)} %get-tuple-element.13.place_ref, ...), custom_call_target="tpu_custom_call" | custom-call | tf_op jit(solution)/shard_map/pallas_call | solution.py:438
Async XLA Ops:
  0.0 1.3 %copy-start = (bf16[3,4,96,512]{3,2,1,0:T(8,128)(2,1)S(1)}, bf16[3,4,96,512]{3,2,1,0:T(8,128)(2,1)}, u32[]{:S(2)}) copy-start(bf16[3,4,96,512]{3,2,1,0:T(8,128)(2,1)} %x_ref.1) | copy-start | bytes 3538948
  1.3 0.7 %copy-start.1 = (s32[4,16]{1,0:T(4,128)S(1)}, s32[4,16]{1,0:T(4,128)}, u32[]{:S(2)}) copy-start(s32[4,16]{1,0:T(4,128)} %zonal_ref.1) | copy-start | bytes 772
  2.0 0.7 %copy-start.2 = (s32[4,16]{1,0:T(4,128)S(1)}, s32[4,16]{1,0:T(4,128)}, u32[]{:S(2)}) copy-start(s32[4,16]{1,0:T(4,128)} %meridional_ref.1) | copy-start | bytes 772
  2.6 0.7 %copy-start.3 = (s32[4,16]{1,0:T(4,128)S(1)}, s32[4,16]{1,0:T(4,128)}, u32[]{:S(2)}) copy-start(s32[4,16]{1,0:T(4,128)} %codes_ref.1) | copy-start | bytes 772

commit v3 on v2

--- a/solution.py
+++ b/solution.py
@@ -10,6 +10,7 @@
 
 STEPS = 4
 HALO = 2 * STEPS
+WINDOW = 3
 TIME_STEP = 0.15
 FILTER = 0.03
 AMP_UNIT = 0.04
@@ -26,13 +27,34 @@
     return rest * (2.0 * math.pi / count)
 
 
-def waves(me, n, own, nx, width, levels, zonal, meridional, codes):
-    def in_row(x):
-        x = x.astype(jnp.float32)
-        return jnp.concatenate([x[l : l + 1, :] for l in range(levels)], axis=1)
-
-    zonal, meridional, codes = in_row(zonal), in_row(meridional), in_row(codes)
+def in_row(x, levels):
+    x = x.astype(jnp.float32)
+    return jnp.concatenate([x[l : l + 1, :] for l in range(levels)], axis=1)
+
+
+def waves_left(me, nx, width, levels, zonal, codes):
+    zonal, codes = in_row(zonal, levels), in_row(codes, levels)
     count = zonal.shape[1]
+    zonal = jnp.concatenate([zonal, zonal], axis=1)
+    weights = AMP_UNIT * jnp.concatenate([codes, codes], axis=1)
+    wide = width + 2 * HALO
+    shape = (levels * wide, 2 * count)
+    level, x = level_and_column(shape, 0, levels, wide)
+    lane = lax.broadcasted_iota(jnp.int32, shape, 1)
+    lon = x + (me * width - HALO)
+    lon = jnp.where(lon < 0, lon + nx, jnp.where(lon >= nx, lon - nx, lon))
+    phase = turns(lon.astype(jnp.float32) * zonal, float(nx))
+    modes = count // levels
+    sine = lane >= count
+    within = lane - jnp.where(sine, count, 0)
+    own_level = (within >= level * modes) & (within < level * modes + modes)
+    left = jnp.where(sine, -jnp.sin(phase), jnp.cos(phase)) * weights
+    return jnp.where(own_level, left, 0.0)
+
+
+def waves_right(ny, levels, meridional):
+    meridional = in_row(meridional, levels)
+    count = meridional.shape[1]
     square = (count, count)
     diagonal = lax.broadcasted_iota(jnp.int32, square, 0) == lax.broadcasted_iota(
         jnp.int32, square, 1
@@ -40,39 +62,17 @@
     meridional = jnp.sum(
         jnp.where(diagonal, jnp.broadcast_to(meridional, square), 0.0), axis=1, keepdims=True
     )
-    zonal = jnp.concatenate([zonal, zonal], axis=1)
-    weights = AMP_UNIT * jnp.concatenate([codes, codes], axis=1)
-    ny = n * own
-    wide = width + 2 * HALO
-    shape = (levels * wide, 2 * count)
-    row = lax.broadcasted_iota(jnp.int32, shape, 0)
-    lane = lax.broadcasted_iota(jnp.int32, shape, 1)
-    level = jnp.zeros(shape, jnp.int32)
-    for l in range(1, levels):
-        level = level + jnp.where(row >= l * wide, 1, 0)
-    lon = row - level * wide + (me * width - HALO)
-    lon = jnp.where(lon < 0, lon + nx, jnp.where(lon >= nx, lon - nx, lon))
-    phase = turns(lon.astype(jnp.float32) * zonal, float(nx))
-    modes = count // levels
-    sine = lane >= count
-    within = lane - jnp.where(sine, count, 0)
-    own_level = (within >= level * modes) & (within < level * modes + modes)
-    left = jnp.where(sine, -jnp.sin(phase), jnp.cos(phase)) * weights
-    left = jnp.where(own_level, left, 0.0)
     lat = lax.broadcasted_iota(jnp.int32, (count, ny), 1).astype(jnp.float32)
     phase = turns(lat * meridional, float(ny))
-    right = jnp.concatenate([jnp.cos(phase), jnp.sin(phase)], axis=0)
-    return jnp.dot(
-        left, right, preferred_element_type=jnp.float32, precision=lax.Precision.HIGHEST
-    )
+    return jnp.concatenate([jnp.cos(phase), jnp.sin(phase)], axis=0)
 
 
 def gather_kernel(
     n,
-    x_ref,
-    zonal_ref,
-    meridional_ref,
-    codes_ref,
+    x_hbm,
+    zonal_hbm,
+    meridional_hbm,
+    codes_hbm,
     out_ref,
     added_ref,
     mats_ref,
@@ -83,6 +83,13 @@
     recv_sem,
     fsend_sem,
     frecv_sem,
+    x_ref,
+    zonal_ref,
+    meridional_ref,
+    codes_ref,
+    left_ref,
+    right_ref,
+    in_sem,
 ):
     comps, levels, own, nx = x_ref.shape
     width = nx // n
@@ -100,11 +107,31 @@
         )
     pl.semaphore_signal(barrier, inc=1, device_id=(partner, me), device_id_type=MESH)
 
-    cut = ceil_to(total // 2, 16)
-    parts = (pl.ds(0, cut), pl.ds(cut, total - cut))
+    size = total // 2
+    mine = pl.ds(pl.multiple_of(parity * size, 16), size)
+    other = pl.ds(pl.multiple_of((1 - parity) * size, 16), size)
     group = LANES // width
     tiles = nx // LANES
     mine_tile = lax.div(me, group)
+
+    loads = [
+        pltpu.make_async_copy(source, target, in_sem.at[i])
+        for i, (source, target) in enumerate(
+            (
+                (x_hbm, x_ref),
+                (zonal_hbm, zonal_ref),
+                (meridional_hbm, meridional_ref),
+                (codes_hbm, codes_ref),
+            )
+        )
+    ]
+    for load in loads:
+        load.start()
+    for load in loads:
+        load.wait()
+    used = comps * (own + half)
+    if total > used:
+        send_ref[:, used:, :] = jnp.zeros((n, total - used, LANES), jnp.bfloat16)
 
     def flipped(value, bits):
         result = value
@@ -141,7 +168,7 @@
                 start = comps * own + c * half
                 send_ref[t, start : start + half, :] = packed
 
-    def spread(flip, mine):
+    def spread(flip):
         target = flipped(me, flip)
         return pltpu.make_async_remote_copy(
             src_ref=send_ref.at[target, mine],
@@ -152,7 +179,7 @@
             device_id_type=MESH,
         )
 
-    def arrival(flip, mine):
+    def arrival(flip):
         source = flipped(me, flip)
         return pltpu.make_async_remote_copy(
             src_ref=send_ref.at[source, mine],
@@ -177,67 +204,78 @@
     order = []
     for tile_flip in range(tiles - 1, -1, -1):
         pack(flipped(mine_tile, tile_flip))
-        if tile_flip == tiles - 1:
-            pl.semaphore_wait(barrier, n)
         flips = [tile_flip * group + d for d in range(group - 1, -1, -1)]
         flips = [f for f in flips if f]
         order += flips
-        for p in range(2):
-
-            @pl.when(parity == p)
-            def _(p=p, flips=flips):
-                for f in flips:
-                    spread(f, parts[p]).start()
+        if tile_flip == tiles - 1:
+            pl.semaphore_wait(barrier, n)
+            for f in flips[:WINDOW]:
+                spread(f).start()
+        if tile_flip < tiles // 2:
+            for f in flips:
+                spread(f).start()
+    out_ref[me] = send_ref[me]
 
     near = [f for f in order if f < n // 2][::-1]
     far = [f for f in order if f >= n // 2]
 
-    def early(mine):
-        for f in near[: group - 1]:
-            arrival(f, mine).wait_recv()
-            forward(f, mine).start()
-
-    for p in range(2):
-        pl.when(parity == p)(functools.partial(early, parts[p]))
-    out_ref[me] = send_ref[me]
-    place_ref[...] = placing(levels, width)
-    geo_ref[...] = geometry(n * own)
-    base = 0
+    def pass_on(flip):
+        arrival(flip).wait_recv()
+        forward(flip, mine).start()
+
+    starts = [0]
     for step in range(STEPS):
+        rows = levels * (width + 2 * HALO - 4 * step - 4)
+        starts.append(starts[-1] + 5 * rows)
+
+    def matrices(step):
+        base = starts[step]
         for block in stencils(levels, width + 2 * HALO - 4 * step):
             mats_ref[base : base + block.shape[0], : block.shape[1]] = block
             base += block.shape[0]
-    added_ref[...] = waves(
-        me, n, own, nx, width, levels, zonal_ref[...], meridional_ref[...], codes_ref[...]
-    )
-
-    def exchange(mine, other):
-        pending = near[group - 1 :]
-        for i, f in enumerate(far):
-            if i < len(pending):
-                arrival(pending[i], mine).wait_recv()
-                forward(pending[i], mine).start()
-            arrival(f, mine).wait_recv()
-            forward(f, mine).start()
-        for f in order:
-            forward(f, other).wait_recv()
-        for f in order:
-            spread(f, mine).wait_send()
-            forward(f, mine).wait_send()
-
-    @pl.when(parity == 0)
-    def _():
-        exchange(parts[0], parts[1])
-
-    @pl.when(parity == 1)
-    def _():
-        exchange(parts[1], parts[0])
+
+    def small():
+        place_ref[...] = placing(levels, width)
+        geo_ref[...] = geometry(n * own)
+
+    def left():
+        left_ref[...] = waves_left(me, nx, width, levels, zonal_ref[...], codes_ref[...])
+
+    def right():
+        right_ref[...] = waves_right(n * own, levels, meridional_ref[...])
+
+    def added():
+        added_ref[...] = jnp.dot(
+            left_ref[...],
+            right_ref[...],
+            preferred_element_type=jnp.float32,
+            precision=lax.Precision.HIGHEST,
+        )
+
+    pieces = [functools.partial(matrices, step) for step in range(STEPS)]
+    pieces += [small, left, right, added]
+    rounds = len(far)
+    for i, f in enumerate(far):
+        if i < len(near):
+            pass_on(near[i])
+        pass_on(f)
+        spread(f).wait_send()
+        if i + WINDOW < rounds:
+            spread(far[i + WINDOW]).start()
+        for piece in pieces[i * len(pieces) // rounds : (i + 1) * len(pieces) // rounds]:
+            piece()
+    for f in near + far:
+        forward(f, other).wait_recv()
+    for f in near:
+        spread(f).wait_send()
+    for f in near + far:
+        forward(f, mine).wait_send()
 
 
 def gather(analysis, zonal, meridional, codes, n):
     comps, levels, own, nx = analysis.shape
     half = ceil_to(own // 2, 16)
-    total = comps * (own + half)
+    total = ceil_to(comps * (own + half), 32)
     width = nx // n
     rows = levels * (width + 2 * HALO)
     mat_rows = sum(5 * (rows - 4 * levels * (step + 1)) for step in range(STEPS))
@@ -251,10 +289,16 @@
             jax.ShapeDtypeStruct((rows, 2 * LANES), jnp.bfloat16),
             jax.ShapeDtypeStruct((2, n * own), jnp.float32),
         ),
-        in_specs=[vmem] * 4,
+        in_specs=[pl.BlockSpec(memory_space=pltpu.HBM)] * 4,
         out_specs=(vmem,) * 5,
         scratch_shapes=[pltpu.VMEM((n, total, LANES), jnp.bfloat16)]
-        + [pltpu.SemaphoreType.DMA((n,)) for _ in range(4)],
+        + [pltpu.SemaphoreType.DMA((n,)) for _ in range(4)]
+        + [pltpu.VMEM(x.shape, x.dtype) for x in (analysis, zonal, meridional, codes)]
+        + [
+            pltpu.VMEM((rows, 2 * zonal.size), jnp.float32),
+            pltpu.VMEM((2 * zonal.size, n * own), jnp.float32),
+            pltpu.SemaphoreType.DMA((4,)),
+        ],
         compiler_params=pltpu.CompilerParams(
             collective_id=0, has_side_effects=True, vmem_limit_bytes=24 * 2**20
         ),

time: 63.5 us -> 60.7 us (0.956)
  the two profiles are of different devices: /device:TPU:10 before, /device:TPU:0 now
where the time goes in v3:
time: 60.7 us; the launch traced here: 60.5 us
  Pallas kernels  57.1 us (94%)
  local copies, waits for them, and re-layouts  3.31 us (5%)
    pallas_call x1, Pallas kernels, gather(): pl.pallas_call(functools.partial(gather_kernel, n), out_shape=(jax.ShapeD...  35.3 us
    pallas_call x1, Pallas kernels, shards(): pl.pallas_call(functools.partial(steps_kernel, (n, comps, levels, own, ha...  21.8 us
    unnamed x8, local copies, waits for them, and re-layouts  3.31 us

profile of v3, /device:TPU:0, one launch (start us, length us, event | category | flops | bytes accessed | tf_op | source)
XLA Modules:
  0.0 60.5 jit_solution(11890207303694486853)
XLA Ops:
  0.0 0.0 copy-start
  0.0 1.3 %copy-done = bf16[3,4,96,512]{3,2,1,0:T(8,128)(2,1)S(1)} copy-done((bf16[3,4,96,512]{3,2,1,0:T(8,128)(2,1)S(1)}, bf16[3,4,96,512]{3,2,1,0:T(8,128)(2,1)}, u32[]{:S(2)}) %copy-start) | copy-done | bytes 1179672
  1.3 0.0 copy-start.1
  1.3 0.7 %copy-done.1 = s32[4,16]{1,0:T(4,128)S(1)} copy-done((s32[4,16]{1,0:T(4,128)S(1)}, s32[4,16]{1,0:T(4,128)}, u32[]{:S(2)}) %copy-start.1) | copy-done | bytes 280
  2.0 0.0 copy-start.2
  2.0 0.7 %copy-done.2 = s32[4,16]{1,0:T(4,128)S(1)} copy-done((s32[4,16]{1,0:T(4,128)S(1)}, s32[4,16]{1,0:T(4,128)}, u32[]{:S(2)}) %copy-start.2) | copy-done | bytes 280
  2.6 0.0 copy-start.3
  2.6 0.7 %copy-done.3 = s32[4,16]{1,0:T(4,128)S(1)} copy-done((s32[4,16]{1,0:T(4,128)S(1)}, s32[4,16]{1,0:T(4,128)}, u32[]{:S(2)}) %copy-start.3) | copy-done | bytes 280
  3.3 35.3 %shard_map.46 = (bf16[16,448,128]{2,1,0:T(8,128)(2,1)S(1)}, f32[192,1536]{1,0:T(8,128)S(1)}, bf16[3040,192]{1,0:T(8,128)(2,1)S(1)}, bf16[192,256]{1,0:T(8,128)(2,1)S(1)}, f32[2,1536]{1,0:T(2,128)S(1)}) custom-call(bf16[3,4,96,512]{3,2,1,0:T(8,128)(2,1)S(1)} %copy-done, s32[4,16]{1,0:T(4,128)S(1)} %copy-done.1, s32[4,16]{1,0:T(4,128)S(1)} %copy-done.2, ...), custom_call_target="tpu_custom_call" | custom-call | tf_op jit(solution)/shard_map/pallas_call | solution.py:283
  38.6 21.8 %shard_map.47 = bf16[3,128,1536]{2,1,0:T(8,128)(2,1)} custom-call(bf16[16,448,128]{2,1,0:T(8,128)(2,1)S(1)} %get-tuple-element.10.r_ref, f32[192,1536]{1,0:T(8,128)S(1)} %get-tuple-element.11.added_ref, bf16[3040,192]{1,0:T(8,128)(2,1)S(1)} %get-tuple-element.12.mats_ref, bf16[192,256]{1,0:T(8,128)(2,1)S(1)} %get-tuple-element.13.place_ref, ...), custom_call_target="tpu_custom_call" | custom-call | tf_op jit(solution)/shard_map/pallas_call | solution.py:482
Async XLA Ops:
  0.0 1.3 %copy-start = (bf16[3,4,96,512]{3,2,1,0:T(8,128)(2,1)S(1)}, bf16[3,4,96,512]{3,2,1,0:T(8,128)(2,1)}, u32[]{:S(2)}) copy-start(bf16[3,4,96,512]{3,2,1,0:T(8,128)(2,1)} %x_hbm.1) | copy-start | bytes 3538948
  1.3 0.7 %copy-start.1 = (s32[4,16]{1,0:T(4,128)S(1)}, s32[4,16]{1,0:T(4,128)}, u32[]{:S(2)}) copy-start(s32[4,16]{1,0:T(4,128)} %zonal_hbm.1) | copy-start | bytes 772
  2.0 0.7 %copy-start.2 = (s32[4,16]{1,0:T(4,128)S(1)}, s32[4,16]{1,0:T(4,128)}, u32[]{:S(2)}) copy-start(s32[4,16]{1,0:T(4,128)} %meridional_hbm.1) | copy-start | bytes 772
  2.6 0.7 %copy-start.3 = (s32[4,16]{1,0:T(4,128)S(1)}, s32[4,16]{1,0:T(4,128)}, u32[]{:S(2)}) copy-start(s32[4,16]{1,0:T(4,128)} %codes_hbm.1) | copy-start | bytes 772

commit v4 on v3

--- a/solution.py
+++ b/solution.py
@@ -70,10 +70,9 @@
 def gather_kernel(
     n,
     x_hbm,
-    zonal_hbm,
-    meridional_hbm,
-    codes_hbm,
+    waves_hbm,
     out_ref,
+    mate_ref,
     added_ref,
     mats_ref,
     place_ref,
@@ -83,10 +82,10 @@
     recv_sem,
     fsend_sem,
     frecv_sem,
+    msend_sem,
+    mrecv_sem,
     x_ref,
-    zonal_ref,
-    meridional_ref,
-    codes_ref,
+    waves_ref,
     left_ref,
     right_ref,
     in_sem,
@@ -94,7 +93,6 @@
     comps, levels, own, nx = x_ref.shape
     width = nx // n
     total = out_ref.shape[1]
-    half = ceil_to(own // 2, 16)
     me = lax.axis_index("gx")
     member = lax.axis_index("member")
     parity = lax.rem(member, 2)
@@ -117,19 +115,14 @@
     loads = [
         pltpu.make_async_copy(source, target, in_sem.at[i])
         for i, (source, target) in enumerate(
-            (
-                (x_hbm, x_ref),
-                (zonal_hbm, zonal_ref),
-                (meridional_hbm, meridional_ref),
-                (codes_hbm, codes_ref),
-            )
+            ((x_hbm, x_ref), (waves_hbm, waves_ref))
         )
     ]
     for load in loads:
         load.start()
     for load in loads:
         load.wait()
-    used = comps * (own + half)
+    used = (comps + 1) * own
     if total > used:
         send_ref[:, used:, :] = jnp.zeros((n, total - used, LANES), jnp.bfloat16)
 
@@ -149,6 +142,7 @@
     def pack(tile):
         before = lax.rem(tile + tiles - 1, tiles)
         after = lax.rem(tile + 1, tiles)
+        edges = [[] for _ in range(group)]
         for c in range(comps):
             here = tile_columns(c, tile)
             low = [x[:, LANES - HALO :] for x in tile_columns(c, before)]
@@ -159,14 +153,15 @@
                 last = first + width
                 main = [x[:, first:last] for x in here]
                 send_ref[t, c * own : (c + 1) * own, :] = jnp.concatenate(main, axis=1)
-                edges = []
                 for l in range(levels):
-                    edges.append(here[l][:, first - HALO : first] if d else low[l])
-                    edges.append(here[l][:, last : last + HALO] if last < LANES else high[l])
-                edge = jnp.concatenate(edges, axis=1)
-                packed = jnp.concatenate([edge[:half], edge[own - half :]], axis=1)
-                start = comps * own + c * half
-                send_ref[t, start : start + half, :] = packed
+                    if d % 2 == 0:
+                        edges[d].append(here[l][:, first - HALO : first] if d else low[l])
+                    else:
+                        edges[d].append(here[l][:, last : last + HALO] if last < LANES else high[l])
+        blank = jnp.zeros((own, LANES - comps * levels * HALO), jnp.bfloat16)
+        for d in range(group):
+            edge = jnp.concatenate(edges[d] + [blank], axis=1)
+            send_ref[tile * group + d, comps * own : (comps + 1) * own, :] = edge
 
     def spread(flip):
         target = flipped(me, flip)
@@ -200,6 +195,22 @@
             device_id=(partner, me),
             device_id_type=MESH,
         )
+
+    mate = flipped(me, 1)
+
+    def share(flip, rows, kind, from_me):
+        owner = me if from_me else mate
+        source = flipped(owner, flip)
+        return pltpu.make_async_remote_copy(
+            src_ref=out_ref.at[source, rows],
+            dst_ref=mate_ref.at[source, rows],
+            send_sem=msend_sem.at[kind, flip],
+            recv_sem=mrecv_sem.at[kind, flip],
+            device_id=(member, mate),
+            device_id_type=MESH,
+        )
+
+    whole = pl.ds(0, total)
 
     order = []
     for tile_flip in range(tiles - 1, -1, -1):
@@ -215,6 +226,7 @@
             for f in flips:
                 spread(f).start()
     out_ref[me] = send_ref[me]
+    share(0, whole, 0, True).start()
 
     near = [f for f in order if f < n // 2][::-1]
     far = [f for f in order if f >= n // 2]
@@ -222,6 +234,7 @@
     def pass_on(flip):
         arrival(flip).wait_recv()
         forward(flip, mine).start()
+        share(flip, mine, 0, True).start()
 
     starts = [0]
     for step in range(STEPS):
@@ -235,14 +248,14 @@
             base += block.shape[0]
 
     def small():
-        place_ref[...] = placing(levels, width)
+        place_ref[...] = placing(comps, levels, width, lax.rem(me, 2))
         geo_ref[...] = geometry(n * own)
 
     def left():
-        left_ref[...] = waves_left(me, nx, width, levels, zonal_ref[...], codes_ref[...])
+        left_ref[...] = waves_left(me, nx, width, levels, waves_ref[:levels], waves_ref[2 * levels :])
 
     def right():
-        right_ref[...] = waves_right(n * own, levels, meridional_ref[...])
+        right_ref[...] = waves_right(n * own, levels, waves_ref[levels : 2 * levels])
 
     def added():
         added_ref[...] = jnp.dot(
@@ -266,17 +279,25 @@
             piece()
     for f in near + far:
         forward(f, other).wait_recv()
+        share(f, other, 1, True).start()
     for f in near:
         spread(f).wait_send()
     for f in near + far:
         forward(f, mine).wait_send()
+    share(0, whole, 0, False).wait_recv()
+    share(0, whole, 0, True).wait_send()
+    for f in near + far:
+        share(f, mine, 0, False).wait_recv()
+        share(f, mine, 0, True).wait_send()
+        share(f, other, 1, False).wait_recv()
+        share(f, other, 1, True).wait_send()
 
 
 def gather(analysis, zonal, meridional, codes, n):
     comps, levels, own, nx = analysis.shape
-    half = ceil_to(own // 2, 16)
-    total = ceil_to(comps * (own + half), 32)
+    total = ceil_to((comps + 1) * own, 32)
     width = nx // n
+    waves = jnp.concatenate([zonal, meridional, codes], axis=0)
     rows = levels * (width + 2 * HALO)
     mat_rows = sum(5 * (rows - 4 * levels * (step + 1)) for step in range(STEPS))
     vmem = pl.BlockSpec(memory_space=pltpu.VMEM)
@@ -284,25 +305,27 @@
         functools.partial(gather_kernel, n),
         out_shape=(
             jax.ShapeDtypeStruct((n, total, LANES), jnp.bfloat16),
+            jax.ShapeDtypeStruct((n, total, LANES), jnp.bfloat16),
             jax.ShapeDtypeStruct((rows, n * own), jnp.float32),
             jax.ShapeDtypeStruct((mat_rows, rows), jnp.bfloat16),
-            jax.ShapeDtypeStruct((rows, 2 * LANES), jnp.bfloat16),
+            jax.ShapeDtypeStruct((comps * rows, 3 * LANES), jnp.bfloat16),
             jax.ShapeDtypeStruct((2, n * own), jnp.float32),
         ),
-        in_specs=[pl.BlockSpec(memory_space=pltpu.HBM)] * 4,
-        out_specs=(vmem,) * 5,
+        in_specs=[pl.BlockSpec(memory_space=pltpu.HBM)] * 2,
+        out_specs=(vmem,) * 6,
         scratch_shapes=[pltpu.VMEM((n, total, LANES), jnp.bfloat16)]
         + [pltpu.SemaphoreType.DMA((n,)) for _ in range(4)]
-        + [pltpu.VMEM(x.shape, x.dtype) for x in (analysis, zonal, meridional, codes)]
+        + [pltpu.SemaphoreType.DMA((2, n)) for _ in range(2)]
+        + [pltpu.VMEM(x.shape, x.dtype) for x in (analysis, waves)]
         + [
             pltpu.VMEM((rows, 2 * zonal.size), jnp.float32),
             pltpu.VMEM((2 * zonal.size, n * own), jnp.float32),
-            pltpu.SemaphoreType.DMA((4,)),
+            pltpu.SemaphoreType.DMA((2,)),
         ],
         compiler_params=pltpu.CompilerParams(
             collective_id=0, has_side_effects=True, vmem_limit_bytes=24 * 2**20
         ),
-    )(analysis, zonal, meridional, codes)
+    )(analysis, waves)
 
 
 def level_and_column(shape, axis, levels, wide):
@@ -313,18 +336,22 @@
     return level, index - level * wide
 
 
-def placing(levels, width):
+def placing(comps, levels, width, odd):
     wide = width + 2 * HALO
-    shape = (levels * wide, 2 * LANES)
-    level, x = level_and_column(shape, 0, levels, wide)
+    shape = (comps * levels * wide, 3 * LANES)
+    field, x = level_and_column(shape, 0, comps * levels, wide)
+    comp, level = level_and_column(shape, 0, comps, levels * wide)
+    level = field - comp * levels
     lane = lax.broadcasted_iota(jnp.int32, shape, 1)
-    inside = (x >= HALO) & (x < HALO + width)
     main = level * width + x - HALO
-    edge = LANES + level * 2 * HALO + jnp.where(x < HALO, x, x - width)
-    hit = (lane == jnp.where(inside, main, edge)) | (
-        jnp.logical_not(inside) & (lane == edge + LANES // 2)
-    )
-    return jnp.where(hit, 1.0, 0.0).astype(jnp.bfloat16)
+    edge_low = LANES + field * HALO + x
+    edge_high = LANES + field * HALO + x - HALO - width
+    mate_low = 2 * LANES + level * width + width - HALO + x
+    mate_high = 2 * LANES + level * width + x - HALO - width
+    low = jnp.where(odd == 1, mate_low, edge_low)
+    high = jnp.where(odd == 1, edge_high, mate_high)
+    wanted = jnp.where(x < HALO, low, jnp.where(x < HALO + width, main, high))
+    return jnp.where(lane == wanted, 1.0, 0.0).astype(jnp.bfloat16)
 
 
 def stencils(levels, wide):
@@ -354,30 +381,24 @@
     return jnp.concatenate([1.0 / jnp.cos(lat), (2.0 * TIME_STEP) * jnp.sin(lat)], axis=0)
 
 
-def steps_kernel(dims, r_ref, added_ref, mats_ref, place_ref, geo_ref, out_ref, *refs):
-    n, comps, levels, own, half, width = dims
+def steps_kernel(dims, r_ref, mate_ref, added_ref, mats_ref, place_ref, geo_ref, out_ref, *refs):
+    n, comps, levels, own, width = dims
     state_ref, hu_ref, wu_ref, wv_ref, wh_ref, wf_ref = refs
     ny = n * own
     wide = width + 2 * HALO
     rows = levels * wide
     pad = wu_ref.shape[1]
 
-    row_index = lax.broadcasted_iota(jnp.int32, (n, 2 * half, LANES), 1)
-    lane_index = lax.broadcasted_iota(jnp.int32, (n, 2 * half, LANES), 2)
-    keep = (row_index < half) == (lane_index < LANES // 2)
+    edge = r_ref[:, comps * own : (comps + 1) * own, :]
     for c in range(comps):
         main = r_ref[:, c * own : (c + 1) * own, :]
-        start = comps * own + c * half
-        edge = r_ref[:, start : start + half, :]
-        both = jnp.concatenate([edge, edge], axis=1)
-        both = jnp.where(keep, both, jnp.zeros_like(both))
-        if 2 * half > own:
-            both = jnp.concatenate(
-                [both[:, : own - half], both[:, half:]], axis=1
-            )
-        block = jnp.concatenate([main, both], axis=2).reshape(ny, 2 * LANES)
+        mate = mate_ref[:, c * own : (c + 1) * own, :]
+        block = jnp.concatenate([main, edge, mate], axis=2).reshape(ny, 3 * LANES)
         field = lax.dot_general(
-            place_ref[...], block, (((1,), (1,)), ((), ())), preferred_element_type=jnp.float32
+            place_ref[c * rows : (c + 1) * rows, :],
+            block,
+            (((1,), (1,)), ((), ())),
+            preferred_element_type=jnp.float32,
         )
         if c == 0:
             field = field + added_ref[...]
@@ -473,16 +494,15 @@
         ny = n * own
         width = nx // n
         wide = width + 2 * HALO
-        half = ceil_to(own // 2, 16)
         gathered = gather(analysis, zonal, meridional, codes, n)
         rows_in = levels * wide
         rows_out = rows_in - 4 * levels
         pad = ny + LANES
         vmem = pl.BlockSpec(memory_space=pltpu.VMEM)
         out = pl.pallas_call(
-            functools.partial(steps_kernel, (n, comps, levels, own, half, width)),
+            functools.partial(steps_kernel, (n, comps, levels, own, width)),
             out_shape=jax.ShapeDtypeStruct((comps, levels * width, ny), jnp.bfloat16),
-            in_specs=[vmem] * 5,
+            in_specs=[vmem] * 6,
             out_specs=vmem,
             scratch_shapes=[
                 pltpu.VMEM((comps, rows_in, ny), jnp.bfloat16),

time: 60.7 us -> 59.1 us (0.974)
  Pallas kernels: 57.1 us -> 55.7 us
  local copies, waits for them, and re-layouts: 3.31 us -> 2.43 us
  other arithmetic: 0 us -> 0.72 us
    pallas_call x1, Pallas kernels: 35.3 us -> 32 us  [gather(): pl.pallas_call(functools.partial(gather_kernel, n), out_shape=(jax.ShapeD...]
    pallas_call x1, Pallas kernels: 21.8 us -> 23.7 us  [shards(): pl.pallas_call(functools.partial(steps_kernel, (n, comps, levels, own, wi...]
    unnamed x8 -> x4, local copies, waits for them, and re-layouts: 3.31 us -> 2.43 us
    concatenate x0 -> x1, other arithmetic: none -> 0.72 us  [gather(): waves = jnp.concatenate([zonal, meridional, codes], axis=0)]
where the time goes in v4:
time: 59.1 us; the launch traced here: 58.9 us
  Pallas kernels  55.7 us (94%)
  local copies, waits for them, and re-layouts  2.43 us (4%)
  other arithmetic  0.72 us (1%)
    pallas_call x1, Pallas kernels, gather(): pl.pallas_call(functools.partial(gather_kernel, n), out_shape=(jax.ShapeD...  32 us
    pallas_call x1, Pallas kernels, shards(): pl.pallas_call(functools.partial(steps_kernel, (n, comps, levels, own, wi...  23.7 us
    unnamed x4, local copies, waits for them, and re-layouts  2.43 us

profile of v4, /device:TPU:0, one launch (start us, length us, event | category | flops | bytes accessed | tf_op | source)
XLA Modules:
  0.0 58.9 jit_solution(1194038898623612284)
XLA Ops:
  0.0 0.7 %pad_add_fusion.waves_hbm = s32[12,16]{1,0:T(8,128)S(1)} fusion(s32[4,16]{1,0:T(4,128)} %param.7, s32[4,16]{1,0:T(4,128)} %param.6, s32[4,16]{1,0:T(4,128)} %param.5), kind=kLoop, calls=%fused_computation | loop fusion | flops 384 | bytes 1536 | tf_op jit(solution)/shard_map/concatenate | solution.py:300
  0.7 0.0 copy-start.1
  0.7 1.3 %copy-done.1 = bf16[3,4,96,512]{3,2,1,0:T(8,128)(2,1)S(1)} copy-done((bf16[3,4,96,512]{3,2,1,0:T(8,128)(2,1)S(1)}, bf16[3,4,96,512]{3,2,1,0:T(8,128)(2,1)}, u32[]{:S(2)}) %copy-start.1) | copy-done | bytes 1179672
  2.0 32.0 %shard_map.46 = (bf16[16,384,128]{2,1,0:T(8,128)(2,1)S(1)}, bf16[16,384,128]{2,1,0:T(8,128)(2,1)S(1)}, f32[192,1536]{1,0:T(8,128)S(1)}, bf16[3040,192]{1,0:T(8,1...) custom-call(bf16[3,4,96,512]{3,2,1,0:T(8,128)(2,1)S(1)} %copy-done.1, s32[12,16]{1,0:T(8,128)S(1)} %pad_add_fusion.waves_hbm), custom_call_target="tpu_custom_call" | custom-call | tf_op jit(solution)/shard_map/pallas_call | solution.py:304
  34.0 0.0 copy-start
  34.0 1.2 %copy-done = bf16[16,384,128]{2,1,0:T(8,128)(2,1)} copy-done((bf16[16,384,128]{2,1,0:T(8,128)(2,1)}, bf16[16,384,128]{2,1,0:T(8,128)(2,1)S(1)}, u32[]{:S(2)}) %copy-start) | copy-done | bytes 1572888
  35.2 23.7 %shard_map.47 = bf16[3,128,1536]{2,1,0:T(8,128)(2,1)} custom-call(bf16[16,384,128]{2,1,0:T(8,128)(2,1)S(1)} %get-tuple-element.11.r_ref, bf16[16,384,128]{2,1,0:T(8,128)(2,1)} %copy-done, f32[192,1536]{1,0:T(8,128)S(1)} %get-tuple-element.13.added_ref, bf16[3040,192]{1,0:T(8,128)(2,1)S(1)} %get-tuple-element.14.mats_ref, ...), custom_call_target="tpu_custom_call" | custom-call | tf_op jit(solution)/shard_map/pallas_call | solution.py:502
Async XLA Ops:
  0.7 1.3 %copy-start.1 = (bf16[3,4,96,512]{3,2,1,0:T(8,128)(2,1)S(1)}, bf16[3,4,96,512]{3,2,1,0:T(8,128)(2,1)}, u32[]{:S(2)}) copy-start(bf16[3,4,96,512]{3,2,1,0:T(8,128)(2,1)} %x_hbm.1) | copy-start | bytes 3538948
  34.0 1.2 %copy-start = (bf16[16,384,128]{2,1,0:T(8,128)(2,1)}, bf16[16,384,128]{2,1,0:T(8,128)(2,1)S(1)}, u32[]{:S(2)}) copy-start(bf16[16,384,128]{2,1,0:T(8,128)(2,1)S(1)} %get-tuple-element.12.mate_ref) | copy-start | bytes 4718596

commit v5 on v4

--- a/solution.py
+++ b/solution.py
@@ -11,6 +11,7 @@
 STEPS = 4
 HALO = 2 * STEPS
 WINDOW = 3
+COLUMNS = 256
 TIME_STEP = 0.15
 FILTER = 0.03
 AMP_UNIT = 0.04
@@ -69,8 +70,8 @@
 
 def gather_kernel(
     n,
-    x_hbm,
-    waves_hbm,
+    x_ref,
+    waves_ref,
     out_ref,
     mate_ref,
     added_ref,
@@ -84,11 +85,8 @@
     frecv_sem,
     msend_sem,
     mrecv_sem,
-    x_ref,
-    waves_ref,
     left_ref,
     right_ref,
-    in_sem,
 ):
     comps, levels, own, nx = x_ref.shape
     width = nx // n
@@ -112,16 +110,6 @@
     tiles = nx // LANES
     mine_tile = lax.div(me, group)
 
-    loads = [
-        pltpu.make_async_copy(source, target, in_sem.at[i])
-        for i, (source, target) in enumerate(
-            ((x_hbm, x_ref), (waves_hbm, waves_ref))
-        )
-    ]
-    for load in loads:
-        load.start()
-    for load in loads:
-        load.wait()
     used = (comps + 1) * own
     if total > used:
         send_ref[:, used:, :] = jnp.zeros((n, total - used, LANES), jnp.bfloat16)
@@ -311,16 +299,14 @@
             jax.ShapeDtypeStruct((comps * rows, 3 * LANES), jnp.bfloat16),
             jax.ShapeDtypeStruct((2, n * own), jnp.float32),
         ),
-        in_specs=[pl.BlockSpec(memory_space=pltpu.HBM)] * 2,
+        in_specs=[vmem] * 2,
         out_specs=(vmem,) * 6,
         scratch_shapes=[pltpu.VMEM((n, total, LANES), jnp.bfloat16)]
         + [pltpu.SemaphoreType.DMA((n,)) for _ in range(4)]
         + [pltpu.SemaphoreType.DMA((2, n)) for _ in range(2)]
-        + [pltpu.VMEM(x.shape, x.dtype) for x in (analysis, waves)]
         + [
             pltpu.VMEM((rows, 2 * zonal.size), jnp.float32),
             pltpu.VMEM((2 * zonal.size, n * own), jnp.float32),
-            pltpu.SemaphoreType.DMA((2,)),
         ],
         compiler_params=pltpu.CompilerParams(
             collective_id=0, has_side_effects=True, vmem_limit_bytes=24 * 2**20
@@ -383,7 +369,7 @@
 
 def steps_kernel(dims, r_ref, mate_ref, added_ref, mats_ref, place_ref, geo_ref, out_ref, *refs):
     n, comps, levels, own, width = dims
-    state_ref, hu_ref, wu_ref, wv_ref, wh_ref, wf_ref = refs
+    state_ref, hu_ref, wu_ref, wv_ref, wh_ref, wf_ref, inv_ref = refs
     ny = n * own
     wide = width + 2 * HALO
     rows = levels * wide
@@ -407,6 +393,7 @@
     for ref in (wu_ref, wv_ref, wh_ref):
         ref[:, ny:] = jnp.zeros((ref.shape[0], pad - ny), jnp.bfloat16)
 
+    inv_ref[...] = jnp.broadcast_to(geo_ref[0:1, :], (16, ny)).astype(jnp.bfloat16)
     base = 0
     for step in range(STEPS):
         rows_in = levels * (wide - 4 * step)
@@ -422,14 +409,16 @@
         )
 
         def times(matrix, x, into):
-            into[: matrix.shape[0], :ny] = jnp.dot(
-                matrix, x, preferred_element_type=jnp.float32
-            ).astype(jnp.bfloat16)
-
-        times(wind, state_ref[1, :rows_in, :], wu_ref)
-        times(wind, state_ref[2, :rows_in, :], wv_ref)
-        times(thick, state_ref[0, :rows_in, :], wh_ref)
-        times(flux, hu_ref[:rows_in, :], wf_ref)
+            for first in range(0, ny, COLUMNS):
+                last = min(ny, first + COLUMNS)
+                into[: matrix.shape[0], first:last] = jnp.dot(
+                    matrix, x[:rows_in, first:last], preferred_element_type=jnp.float32
+                ).astype(jnp.bfloat16)
+
+        times(wind, state_ref.at[1], wu_ref)
+        times(wind, state_ref.at[2], wv_ref)
+        times(thick, state_ref.at[0], wh_ref)
+        times(flux, hu_ref, wf_ref)
 
         def group(g, carry, rows_out=rows_out, last=step == STEPS - 1):
             size = 16
@@ -447,7 +436,7 @@
             def fourth(x, near):
                 return ((near[0] + near[3]) - 4.0 * (near[1] + near[2]) + 6.0 * x)[:, :ny]
 
-            inv = jnp.broadcast_to(geo_ref[0:1, :], (size, ny)).astype(jnp.bfloat16)
+            inv = inv_ref[...]
             cor = geo_ref[1:2, :]
             h, u, v, p = (
                 part(wh_ref, 0, pad),
@@ -511,8 +500,9 @@
                 pltpu.VMEM((3 * rows_out, pad), jnp.bfloat16),
                 pltpu.VMEM((4 * rows_out, pad), jnp.bfloat16),
                 pltpu.VMEM((rows_out, ny), jnp.bfloat16),
+                pltpu.VMEM((16, ny), jnp.bfloat16),
             ],
-            compiler_params=pltpu.CompilerParams(vmem_limit_bytes=48 * 2**20),
+            compiler_params=pltpu.CompilerParams(vmem_limit_bytes=32 * 2**20),
         )(*gathered)
         return out.reshape(comps, levels, width, ny)
 

time: 59.1 us -> 56.3 us (0.953)
  Pallas kernels: 55.7 us -> 54.1 us
  local copies, waits for them, and re-layouts: 2.43 us -> 1.27 us
    pallas_call x1, Pallas kernels: 23.7 us -> 22.3 us  [shards(): pl.pallas_call(functools.partial(steps_kernel, (n, comps, levels, own, wi...]
    unnamed x4 -> x2, local copies, waits for them, and re-layouts: 2.43 us -> 1.27 us
where the time goes in v5:
time: 56.3 us; the launch traced here: 56.1 us
  Pallas kernels  54.1 us (96%)
  local copies, waits for them, and re-layouts  1.27 us (2%)
  other arithmetic  0.72 us (1%)
    pallas_call x1, Pallas kernels, gather(): pl.pallas_call(functools.partial(gather_kernel, n), out_shape=(jax.ShapeD...  31.9 us
    pallas_call x1, Pallas kernels, shards(): pl.pallas_call(functools.partial(steps_kernel, (n, comps, levels, own, wi...  22.3 us
    unnamed x2, local copies, waits for them, and re-layouts  1.27 us

profile of v5, /device:TPU:0, one launch (start us, length us, event | category | flops | bytes accessed | tf_op | source)
XLA Modules:
  0.0 56.1 jit_solution(7838410802237441205)
XLA Ops:
  0.0 0.7 %pad_add_fusion.waves_ref = s32[12,16]{1,0:T(8,128)S(1)} fusion(s32[4,16]{1,0:T(4,128)} %param.7, s32[4,16]{1,0:T(4,128)} %param.6, s32[4,16]{1,0:T(4,128)} %param.5), kind=kLoop, calls=%fused_computation | loop fusion | flops 384 | bytes 1536 | tf_op jit(solution)/shard_map/concatenate | solution.py:288
  0.7 0.0 copy-start
  0.7 1.3 %copy-done = bf16[3,4,96,512]{3,2,1,0:T(8,128)(2,1)S(1)} copy-done((bf16[3,4,96,512]{3,2,1,0:T(8,128)(2,1)S(1)}, bf16[3,4,96,512]{3,2,1,0:T(8,128)(2,1)}, u32[]{:S(2)}) %copy-start) | copy-done | bytes 1179672
  2.0 31.9 %shard_map.46 = (bf16[16,384,128]{2,1,0:T(8,128)(2,1)S(1)}, bf16[16,384,128]{2,1,0:T(8,128)(2,1)S(1)}, f32[192,1536]{1,0:T(8,128)S(1)}, bf16[3040,192]{1,0:T(8,1...) custom-call(bf16[3,4,96,512]{3,2,1,0:T(8,128)(2,1)S(1)} %copy-done, s32[12,16]{1,0:T(8,128)S(1)} %pad_add_fusion.waves_ref), custom_call_target="tpu_custom_call" | custom-call | tf_op jit(solution)/shard_map/pallas_call | solution.py:292
  33.9 22.3 %shard_map.47 = bf16[3,128,1536]{2,1,0:T(8,128)(2,1)} custom-call(bf16[16,384,128]{2,1,0:T(8,128)(2,1)S(1)} %get-tuple-element.11.r_ref, bf16[16,384,128]{2,1,0:T(8,128)(2,1)S(1)} %get-tuple-element.12.mate_ref, f32[192,1536]{1,0:T(8,128)S(1)} %get-tuple-element.13.added_ref, bf16[3040,192]{1,0:T(8,128)(2,1)S(1)} %get-tuple-element.14.mats_ref, ...), custom_call_target="tpu_custom_call" | custom-call | tf_op jit(solution)/shard_map/pallas_call | solution.py:491
Async XLA Ops:
  0.7 1.3 %copy-start = (bf16[3,4,96,512]{3,2,1,0:T(8,128)(2,1)S(1)}, bf16[3,4,96,512]{3,2,1,0:T(8,128)(2,1)}, u32[]{:S(2)}) copy-start(bf16[3,4,96,512]{3,2,1,0:T(8,128)(2,1)} %x_ref.1) | copy-start | bytes 3538948

commit v6 on v5

--- a/solution.py
+++ b/solution.py
@@ -10,7 +10,7 @@
 
 STEPS = 4
 HALO = 2 * STEPS
-WINDOW = 3
+WINDOW = 4
 COLUMNS = 256
 TIME_STEP = 0.15
 FILTER = 0.03

time: 56.3 us -> 56 us (level)
  no operation moved by 1% of the time
where the time goes in v6:
time: 56 us; the launch traced here: 55.9 us
  Pallas kernels  53.9 us (96%)
  local copies, waits for them, and re-layouts  1.27 us (2%)
  other arithmetic  0.72 us (1%)
    pallas_call x1, Pallas kernels, gather(): pl.pallas_call(functools.partial(gather_kernel, n), out_shape=(jax.ShapeD...  31.6 us
    pallas_call x1, Pallas kernels, shards(): pl.pallas_call(functools.partial(steps_kernel, (n, comps, levels, own, wi...  22.3 us
    unnamed x2, local copies, waits for them, and re-layouts  1.27 us

profile of v6, /device:TPU:0, one launch (start us, length us, event | category | flops | bytes accessed | tf_op | source)
XLA Modules:
  0.0 55.9 jit_solution(14858241904977626856)
XLA Ops:
  0.0 0.7 %pad_add_fusion.waves_ref = s32[12,16]{1,0:T(8,128)S(1)} fusion(s32[4,16]{1,0:T(4,128)} %param.7, s32[4,16]{1,0:T(4,128)} %param.6, s32[4,16]{1,0:T(4,128)} %param.5), kind=kLoop, calls=%fused_computation | loop fusion | flops 384 | bytes 1536 | tf_op jit(solution)/shard_map/concatenate | solution.py:288
  0.7 0.0 copy-start
  0.7 1.3 %copy-done = bf16[3,4,96,512]{3,2,1,0:T(8,128)(2,1)S(1)} copy-done((bf16[3,4,96,512]{3,2,1,0:T(8,128)(2,1)S(1)}, bf16[3,4,96,512]{3,2,1,0:T(8,128)(2,1)}, u32[]{:S(2)}) %copy-start) | copy-done | bytes 1179672
  2.0 31.6 %shard_map.46 = (bf16[16,384,128]{2,1,0:T(8,128)(2,1)S(1)}, bf16[16,384,128]{2,1,0:T(8,128)(2,1)S(1)}, f32[192,1536]{1,0:T(8,128)S(1)}, bf16[3040,192]{1,0:T(8,1...) custom-call(bf16[3,4,96,512]{3,2,1,0:T(8,128)(2,1)S(1)} %copy-done, s32[12,16]{1,0:T(8,128)S(1)} %pad_add_fusion.waves_ref), custom_call_target="tpu_custom_call" | custom-call | tf_op jit(solution)/shard_map/pallas_call | solution.py:292
  33.6 22.3 %shard_map.47 = bf16[3,128,1536]{2,1,0:T(8,128)(2,1)} custom-call(bf16[16,384,128]{2,1,0:T(8,128)(2,1)S(1)} %get-tuple-element.11.r_ref, bf16[16,384,128]{2,1,0:T(8,128)(2,1)S(1)} %get-tuple-element.12.mate_ref, f32[192,1536]{1,0:T(8,128)S(1)} %get-tuple-element.13.added_ref, bf16[3040,192]{1,0:T(8,128)(2,1)S(1)} %get-tuple-element.14.mats_ref, ...), custom_call_target="tpu_custom_call" | custom-call | tf_op jit(solution)/shard_map/pallas_call | solution.py:491
Async XLA Ops:
  0.7 1.3 %copy-start = (bf16[3,4,96,512]{3,2,1,0:T(8,128)(2,1)S(1)}, bf16[3,4,96,512]{3,2,1,0:T(8,128)(2,1)}, u32[]{:S(2)}) copy-start(bf16[3,4,96,512]{3,2,1,0:T(8,128)(2,1)} %x_ref.1) | copy-start | bytes 3538948
